TPU v7x, 128 devices: a whole 4x4x4 slice. The times are simulated.
128 devices in a mesh: space: 8 (over z_lo, y), tm: 16 (over z_hi, x, core).
Axes of the slice: x: 4, y: 4, z: 4 (z_hi: 2, z_lo: 2; z = z_hi * 2 + z_lo), core: 2. Of those that a mesh axis runs over, the one named last changes fastest.
Arguments:
- snapshots: bfloat16 [25600, 4096], P('space', 'tm')
- var_index: int32 [25600], P('space'), may hold values from 0 to 7, as said below
- modes: bfloat16 [25600, 64], P('space'), may hold values from -0.0390625 to 0.0390625
- retained: int32 [1], replicated, may hold values from 32 to 64
Outputs:
- gram: float32 [4096, 4096], P(None, 'tm')
- reduced: float32 [64, 4096], P('space', 'tm')
Inputs may be any that keep to these rules, and one draw needn't show every extreme that they name: `var_index`: each variable labels the same number of rows, a 8-th of them.
All inputs are finite; a program needn't handle non-finite values.
Results may differ from a plain program's by a relative error of at most 0.0029.
Values may be sent and summed in bfloat16 or wider, within the bound.
A program may use at most 128 MiB of HBM per device.

v0:
```python
import jax
import jax.numpy as jnp
from jax import lax
from jax.sharding import PartitionSpec as P

VARS = 8


def cross(left, right):
    return lax.dot_general(
        left, right, (((0,), (0,)), ((), ())), preferred_element_type=jnp.float32
    )


def space_total(partial_value):
    return lax.psum(partial_value, "space")


def local(snapshots, var_index, modes, retained):
    rows_dev = snapshots.shape[0]
    snap_dev = snapshots.shape[1]
    n_space = lax.axis_size("space")
    n_time = lax.axis_size("tm")
    total_rows = rows_dev * n_space
    count = total_rows // VARS * (snap_dev * n_time)
    onehot = (var_index[:, None] == jnp.arange(VARS)[None, :]).astype(jnp.float32)
    row_sum = jnp.sum(snapshots, axis=1, dtype=jnp.float32)
    sums = lax.psum(jnp.sum(onehot * row_sum[:, None], axis=0), ("space", "tm"))
    mean = sums / count
    mean_row = jnp.sum(onehot * mean[None, :], axis=1)
    centered = snapshots.astype(jnp.float32) - mean_row[:, None]
    row_sq = jnp.sum(centered * centered, axis=1)
    squares = lax.psum(jnp.sum(onehot * row_sq[:, None], axis=0), ("space", "tm"))
    variance = squares / count
    spread = jnp.sqrt(variance + 1e-06)
    spread_row = jnp.sum(onehot * spread[None, :], axis=1)
    scaled = (centered / spread_row[:, None]).astype(jnp.bfloat16)
    root_rows = jnp.sqrt(jnp.float32(total_rows))
    partial_gram = cross(lax.all_gather(scaled, "tm", axis=1, tiled=True), scaled)
    gram = space_total(partial_gram) / root_rows
    kept = jnp.where(
        jnp.arange(modes.shape[1])[None, :] < retained[0], modes, jnp.zeros_like(modes)
    )
    reduced = lax.psum_scatter(cross(kept, scaled), "space", scatter_dimension=0, tiled=True)
    return (gram, reduced)


def solution(mesh):
    return jax.shard_map(
        local,
        mesh=mesh,
        in_specs=(P("space", "tm"), P("space"), P("space", None), P()),
        out_specs=(P(None, "tm"), P("space", "tm")),
        check_vma=False,
    )
```

profile of v0, /device:TPU:1, one launch (start us, length us, event | category | flops | bytes accessed | tf_op | source)
XLA Modules:
  0.0 474.5 jit_solution(11246445781145687749)
XLA Ops:
  7.2 0.0 copy-start
  7.2 0.0 copy-start.3
  7.2 0.0 all-gather.2.cloned.1.call-start
  7.2 2.1 convert_reduce_fusion
  9.3 0.9 select_reduce_fusion.3
  10.1 68.7 %psum.21 = f32[8]{0:T(128)S(1)} all-reduce(f32[8]{0:T(128)S(1)} %select_reduce_fusion.3), channel_id=1, replica_groups=mesh['space'=8,'tm'=16] {'space','tm'}, use_global_device_ids=true, to_apply=%region_2.0 | all-reduce | flops 8 | bytes 64 | tf_op jit(solution)/shard_map/psum | solution.py:28
  78.8 0.8 select_reduce_fusion.2
  79.7 2.4 fusion.2
  82.0 0.0 copy-done.3
  82.1 0.1 select_reduce_fusion.1
  82.2 62.6 %psum.22 = f32[8]{0:T(128)S(1)} all-reduce(f32[8]{0:T(128)S(1)} %select_reduce_fusion.1), channel_id=1, replica_groups=mesh['space'=8,'tm'=16] {'space','tm'}, use_global_device_ids=true, to_apply=%region_6.0 | all-reduce | flops 8 | bytes 64 | tf_op jit(solution)/shard_map/psum | solution.py:33
  144.8 0.1 select_reduce_fusion
  144.9 0.0 copy-done
  144.9 2.8 fusion.3
  147.8 0.0 all-gather.2.cloned.1.call-update
  147.8 0.0 all-reduce.2.cloned.1.call-start
  147.8 169.9 %all-gather.2.cloned.1.call-done = bf16[3200,4096]{1,0:T(8,128)(2,1)} async-done(((bf16[3200,256]{1,0:T(8,128)(2,1)}), bf16[3200,4096]{1,0:T(8,128)(2,1)}) %all-gather.2.cloned.1.call-update) | async-done | bytes 26214416 | tf_op jit(solution)/shard_map/all_gather | solution.py:39
  317.7 14.4 %fusion.9 = f32[4096,256]{1,0:T(8,128)} fusion(bf16[3200,4096]{1,0:T(8,128)(2,1)} %all-gather.2.cloned.1.call-done, bf16[3200,256]{1,0:T(8,128)(2,1)} %fusion.3), kind=kOutput, calls=%fused_computation.20 | convolution fusion | flops 6710886400 | bytes 32047104 | tf_op jit(solution)/shard_map/dot_general | solution.py:10
  332.1 0.0 copy-start.1
  332.1 0.0 copy-start.2
  332.1 0.0 all-reduce.2.cloned.1.call-update
  332.1 0.0 reduce-scatter.2.cloned.1.call-start
  333.0 0.6 copy-done.1
  333.6 0.1 copy-done.2
  333.6 1.1 fusion.4
  334.7 0.0 reduce-scatter.2.cloned.1.call-update
  334.7 100.0 %all-reduce.2.cloned.1.call-done = f32[4096,256]{1,0:T(8,128)} async-done(((f32[4096,256]{1,0:T(8,128)}), f32[4096,256]{1,0:T(8,128)}) %all-reduce.2.cloned.1.call-update) | async-done | bytes 4194320 | tf_op jit(solution)/shard_map/psum | solution.py:16
  434.7 4.6 broadcast_multiply_fusion
  439.3 28.7 %reduce-scatter.2.cloned.1.call-done = f32[8,256]{1,0:T(8,128)} async-done(((f32[64,256]{1,0:T(8,128)}), f32[8,256]{1,0:T(8,128)}) %reduce-scatter.2.cloned.1.call-update) | async-done | bytes 8208 | tf_op jit(solution)/shard_map/reduce_scatter | solution.py:44
  (3 shorter events, 0.0 us)
Async XLA Ops:
  7.2 137.8 %copy-start = (bf16[3200,256]{1,0:T(8,128)(2,1)S(1)}, bf16[3200,256]{1,0:T(8,128)(2,1)}, u32[]{:S(2)}) copy-start(bf16[3200,256]{1,0:T(8,128)(2,1)} %param.4) | copy-start | bytes 4915204
  7.2 74.9 %copy-start.3 = (s32[3200]{0:T(1024)S(1)}, s32[3200]{0:T(1024)}, u32[]{:S(2)}) copy-start(s32[3200]{0:T(1024)} %param.5) | copy-start | bytes 38404
  7.2 310.5 %all-gather.2.cloned.1.call-start = ((), (), s32[]{:S(2)}) async-start(), calls=%async_computation.1 | async-start | bytes 27852800 | tf_op jit(solution)/shard_map/all_gather | solution.py:39
  147.8 286.9 %all-reduce.2.cloned.1.call-start = ((), (), s32[]{:S(2)}) async-start(), calls=%async_computation.2 | async-start | bytes 8388608 | tf_op jit(solution)/shard_map/psum | solution.py:16
  332.1 1.4 copy-start.1
  332.1 1.5 copy-start.2
  332.1 135.8 %reduce-scatter.2.cloned.1.call-start = ((), (), s32[]{:S(2)}) async-start(), calls=%async_computation.3 | async-start | bytes 73728 | tf_op jit(solution)/shard_map/reduce_scatter | solution.py:44
Sparse Core Ops, SparseCore 0:
  147.9 169.7 all-gather.1
  332.3 102.4 all-reduce.1
  437.6 30.2 reduce-scatter.1
where the time goes:
time: 480 us; the launch traced here: 474 us
  waiting for transfers between devices  299 us (62%)
  blocking collectives  131 us (27%)
  matrix products  15.5 us (3%)
  between operations  14.6 us (3%)
  other arithmetic  13.8 us (3%)
    all_gather x1, waiting for transfers between devices, local(): lax.all_gather(scaled, 'tm', axis=1, tiled=True)  170 us
    psum x1, waiting for transfers between devices, space_total(): return lax.psum(partial_value, 'space')  100 us
    psum x1, blocking collectives, local(): sums = lax.psum(jnp.sum(onehot * row_sum[:, None], axis=0), ('space', 'tm'))  68.7 us
    psum x1, blocking collectives, local(): lax.psum(jnp.sum(onehot * row_sq[:, None], axis=0), ('space', 'tm'))  62.6 us
    reduce_scatter x1, waiting for transfers between devices, local(): lax.psum_scatter(cross(kept, scaled), 'space', scatter_dimension=0, tiled...  28.7 us
    dot_general x2, matrix products, cross(): lax.dot_general(left, right, (((0,), (0,)), ((), ())), preferred_element_...  15.5 us
  transfers between devices with their start and end apart: 3, of which 3 were waited for; matrix products, arithmetic and copies ran while one was open for 1% of the time, Pallas kernels for 0%

commit v1 on v0

v1 whole, which is shorter than its diff:
```python
import jax
import jax.numpy as jnp
from jax import lax
from jax.experimental import pallas as pl
from jax.experimental.pallas import tpu as pltpu
from jax.sharding import PartitionSpec as P

MESH = pl.DeviceIdType.MESH
VARS = 8
NY, NX = 4, 4
NSPACE = 8
F32, BF16 = jnp.float32, jnp.bfloat16


def place():
    s, t = lax.axis_index("space"), lax.axis_index("tm")
    return s // NY, s % NY, t // 8, (t // 2) % NX, t % 2


def at(l, y, h, x, c):
    return (l * NY + y, h * 8 + x * 2 + c)


def nt(a, b):
    return lax.dot_general(a, b, (((1,), (1,)), ((), ())), preferred_element_type=F32)


def merge(tiles):
    n = sum(t[0:8] for t in tiles)
    total = sum(t[8:16] for t in tiles)
    mean = total / jnp.maximum(n, 1.0)
    squares = jnp.zeros_like(n)
    for t in tiles:
        off = t[8:16] / jnp.maximum(t[0:8], 1.0) - mean
        squares = squares + t[16:24] + t[0:8] * off * off
    return n, total, squares


def kernel(count, root, fk, x_ref, vi_ref, modes_ref, ret_ref, gram_ref, red_ref,
           xt, raw, rawe, relay, rawf, sc, sce, scf, hot, mean_l, inv_l, kept,
           tile1, tile2, got1, got2, part, cs, rs, redp, redr, piece, pieceT, ra, rt,
           bulk_s, bulk_r, st1_s, st1_r, st2_s, st2_r, rs_s, rs_r, rd_s, rd_r, ag_s, ra_r, rt_r):
    l, y, h, x, c = place()
    s = l * NY + y
    q = h * 2 + c
    rows = xt.shape[1]
    cols = xt.shape[0]
    ntile = rows // 128

    ring1 = [(dx, dc) for dx in range(NX) for dc in range(2) if (dx, dc) != (0, 0)]
    ring2 = [(dy, dl, dh) for dy in range(NY) for dl in range(2) for dh in range(2) if (dy, dl, dh) != (0, 0, 0)]

    def dev1(dx, dc, sign=1):
        return at(l, y, h, (x + sign * dx + NX) % NX, (c + dc) % 2)

    def dev2(dy, dl, dh, sign=1):
        return at((l + dl) % 2, (y + sign * dy + NY) % NY, (h + dh) % 2, x, c)

    barrier = pltpu.get_barrier_semaphore()
    for d in ring1:
        pl.semaphore_signal(barrier, inc=1, device_id=dev1(*d), device_id_type=MESH)
    for d in ring2:
        pl.semaphore_signal(barrier, inc=1, device_id=dev2(*d), device_id_type=MESH)

    for k in range(ntile):
        xt[:, 128 * k:128 * k + 128] = x_ref[128 * k:128 * k + 128, :].T

    pl.semaphore_wait(barrier, len(ring1) + len(ring2))

    def remote(src, dst, ss, rsem, dev):
        return pltpu.make_async_remote_copy(src, dst, ss, rsem, device_id=dev, device_id_type=MESH)

    fs_mine = pl.multiple_of((x // 2) * (rows - fk), 128)
    half = cols // 2
    to_f = [remote(xt.at[pl.ds(half * k, half), pl.ds(fs_mine, fk)], relay.at[pl.ds(half * k, half)],
                   bulk_s.at[k], bulk_r.at[k], at(l, y, h, (x + NX - 1) % NX, c)) for k in range(2)]
    to_e = remote(xt, rawe, bulk_s.at[2], bulk_r.at[2], at(l, y, h, (x + 1) % NX, c))
    to_z = remote(xt, raw.at[1], bulk_s.at[3], bulk_r.at[3], at(l, y, 1 - h, x, c))
    to_core = remote(xt, raw.at[0], bulk_s.at[4], bulk_r.at[4], at(l, y, h, x, 1 - c))
    for cp in to_f:
        cp.start()
    to_e.start()
    to_z.start()
    to_core.start()

    hot[...] = (vi_ref[...] == lax.broadcasted_iota(jnp.int32, (VARS, rows), 0)).astype(F32)

    def colsum(fn):
        def body(k, acc):
            blk = xt[pl.ds(pl.multiple_of(k * 16, 16), 16), :].astype(F32)
            return acc + fn(blk)
        acc = lax.fori_loop(0, cols // 16, body, jnp.zeros((16, rows), F32))
        return jnp.sum(acc, axis=0, keepdims=True)

    def wide(v):
        return jnp.broadcast_to(v, (VARS, 128))

    n1 = jnp.sum(hot[...], axis=1, keepdims=True) * cols
    sum1 = jnp.sum(hot[...] * colsum(lambda b: b), axis=1, keepdims=True)
    m1 = sum1 / jnp.maximum(n1, 1.0)
    mean_l[...] = jnp.sum(hot[...] * m1, axis=0, keepdims=True)

    def sq(b):
        d = b - mean_l[...]
        return d * d
    sq1 = jnp.sum(hot[...] * colsum(sq), axis=1, keepdims=True)
    tile1[0:8] = wide(n1)
    tile1[8:16] = wide(sum1)
    tile1[16:24] = wide(sq1)
    sends1 = [remote(tile1, got1.at[i], st1_s.at[i], st1_r.at[i], dev1(*d)) for i, d in enumerate(ring1)]
    for cp in sends1:
        cp.start()
    for k in range(ntile):
        kept[:, 128 * k:128 * k + 128] = modes_ref[128 * k:128 * k + 128, :].T
    keep = lax.broadcasted_iota(jnp.int32, kept.shape, 0) < ret_ref[0]
    kept[...] = jnp.where(keep, kept[...].astype(F32), 0.0).astype(BF16)
    for cp in sends1:
        cp.wait_recv()
    n2, sum2, sq2 = merge([tile1[...]] + [got1[i] for i in range(len(ring1))])
    tile2[0:8] = n2
    tile2[8:16] = sum2
    tile2[16:24] = sq2
    sends2 = [remote(tile2, got2.at[i], st2_s.at[i], st2_r.at[i], dev2(*d)) for i, d in enumerate(ring2)]
    for cp in sends2:
        cp.start()
    for cp in sends2:
        cp.wait_recv()
    _, sum3, sq3 = merge([tile2[...]] + [got2[i] for i in range(len(ring2))])
    mean = sum3 / count
    inv = 1.0 / jnp.sqrt(sq3 / count + 1e-06)
    mean_l[...] = jnp.sum(hot[...] * mean[:, 0:1], axis=0, keepdims=True)
    inv_l[...] = jnp.sum(hot[...] * inv[:, 0:1], axis=0, keepdims=True)

    def scale_to(dst, src):
        def body(k, _):
            r = pl.ds(pl.multiple_of(k * 16, 16), 16)
            dst[r, :] = ((src[r, :].astype(F32) - mean_l[...]) * inv_l[...]).astype(BF16)
            return 0
        lax.fori_loop(0, cols // 16, body, 0)

    scale_to(sc.at[q], xt)
    redp[...] = nt(kept[...], sc[q])

    fwd = [remote(relay.at[pl.ds(half * k, half)], rawf.at[pl.ds(half * k, half)],
                  bulk_s.at[5 + k], bulk_r.at[5 + k], at(l, y, h, (x + NX - 1) % NX, c)) for k in range(2)]
    to_core.wait_recv()
    scale_to(sc.at[h * 2 + (1 - c)], raw.at[0])
    for k in range(2):
        to_f[k].wait_recv()
        fwd[k].start()
    to_z.wait_recv()
    to_diag = remote(raw.at[1], raw.at[2], bulk_s.at[7], bulk_r.at[7], at(l, y, h, x, 1 - c))
    to_diag.start()
    scale_to(sc.at[(1 - h) * 2 + c], raw.at[1])
    to_e.wait_recv()
    scale_to(sce, rawe)
    to_diag.wait_recv()
    scale_to(sc.at[(1 - h) * 2 + (1 - c)], raw.at[2])

    def product(kind, right, lanes):
        def body(i, _):
            part[kind, pl.ds(pl.multiple_of(i * cols, cols), cols), :] = nt(sc[i, :, lanes], right)
            return 0
        lax.fori_loop(0, 4, body, 0)

    product(0, sc[q], slice(None))
    product(1, sce[...], slice(None))

    for k in range(2):
        fwd[k].wait_recv()
    fs = pl.multiple_of((((x + 2) % NX) // 2) * (rows - fk), 128)
    fl = pl.ds(fs, fk)
    over = 2 * fk - rows
    first = lax.broadcasted_iota(jnp.int32, (1, fk), 1) < over
    drop = jnp.logical_and(first, x < 2)
    f_inv = jnp.where(drop, 0.0, inv_l[:, fl])

    def fbody(k, _):
        r = pl.ds(pl.multiple_of(k * 16, 16), 16)
        scf[r, :] = ((rawf[r, :].astype(F32) - mean_l[:, fl]) * f_inv).astype(BF16)
        return 0
    lax.fori_loop(0, cols // 16, fbody, 0)
    product(2, scf[...], fl)

    ring3 = [(dl, dy) for dl in range(2) for dy in range(NY) if (dl, dy) != (0, 0)]
    for i in range(NSPACE):
        for kind in range(3):
            cs[i, kind] = part[kind, 128 * i:128 * i + 128, :].astype(BF16)
    rsend, dsend = [], []
    for i, (dl, dy) in enumerate(ring3):
        tl, ty = (l + dl) % 2, (y + dy) % NY
        ts = tl * NY + ty
        rsend.append(remote(cs.at[ts], rs.at[i], rs_s.at[i], rs_r.at[i], at(tl, ty, h, x, c)))
        dsend.append(remote(redp.at[pl.ds(pl.multiple_of(ts * 8, 8), 8)], redr.at[i], rd_s.at[i], rd_r.at[i],
                            at(tl, ty, h, x, c)))
    for a in rsend:
        a.start()
    for a in dsend:
        a.start()
    for a in rsend:
        a.wait_recv()
    for kind in range(3):
        tot = part[kind, pl.ds(pl.multiple_of(s * 128, 128), 128), :]
        for i in range(len(ring3)):
            tot = tot + rs[i, kind].astype(F32)
        tot = tot * (1.0 / root)
        piece[kind] = tot.astype(BF16)
        if kind > 0:
            pieceT[kind - 1] = tot.T.astype(BF16)

    own = s // 2
    oh, oc = own // 2, own % 2
    half_s = s % 2
    agsend = []
    for dl in range(2):
        for dy in range(NY):
            tl, ty = (l + dl) % 2, (y + dy) % NY
            k = dl * NY + dy
            dests = [at(tl, ty, h, x, c), at(tl, ty, h, (x + NX - 1) % NX, c), at(tl, ty, h, (x + 2) % NX, c)]
            for kind in range(3):
                if kind == 0 and k == 0:
                    continue
                cp = remote(piece.at[kind], ra.at[kind, s], ag_s.at[k * 5 + kind], ra_r.at[kind, s], dests[kind])
                cp.start()
                agsend.append(cp)
            for kind in range(2):
                cp = remote(pieceT.at[kind], rt.at[kind, q, half_s], ag_s.at[k * 5 + 3 + kind], rt_r.at[kind, q, half_s],
                            at(tl, ty, oh, x, oc))
                if k == 0:
                    lc = pltpu.make_async_copy(pieceT.at[kind], rt.at[kind, q, half_s], rt_r.at[kind, q, half_s])

                    @pl.when(own == q)
                    def _():
                        lc.start()

                    @pl.when(own != q)
                    def _():
                        cp.start()
                else:
                    cp.start()
                    agsend.append(cp)
    ra[0, s] = piece[0]

    for a in dsend:
        a.wait_recv()
    tot = redp[pl.ds(pl.multiple_of(s * 8, 8), 8), :]
    for i in range(len(ring3)):
        tot = tot + redr[i]
    red_ref[...] = tot

    def got(ref, sem):
        pltpu.make_async_copy(ref, ref, sem).wait()

    def rows_of(hc, xx):
        return ((hc // 2) * 8 + xx * 2 + hc % 2) * cols

    for kind in range(3):
        xx = [x, (x + 1) % NX, (x + 2) % NX][kind]
        for j in range(NSPACE):
            if kind == 0:
                @pl.when(s != j)
                def _():
                    got(ra.at[0, j], ra_r.at[0, j])
            else:
                got(ra.at[kind, j], ra_r.at[kind, j])
            r0 = pl.multiple_of(rows_of(j // 2, xx) + (j % 2) * 128, 128)
            gram_ref[pl.ds(r0, 128), :] = ra[kind, j].astype(F32)
    for kind in range(2):
        xx = [(x + NX - 1) % NX, (x + 2) % NX][kind]
        for hc in range(4):
            r0 = pl.multiple_of(rows_of(hc, xx), cols)
            for b in range(2):
                got(rt.at[kind, hc, b], rt_r.at[kind, hc, b])
                val = rt[kind, hc, b].astype(F32)
                if kind == 1:
                    val = val + gram_ref[pl.ds(r0, cols), 128 * b:128 * b + 128]
                gram_ref[pl.ds(r0, cols), 128 * b:128 * b + 128] = val

    for cp in to_f + fwd + [to_e, to_z, to_core, to_diag] + sends1 + sends2 + rsend + dsend + agsend:
        cp.wait_send()
    for kind in range(2):
        @pl.when(own != q)
        def _():
            remote(pieceT.at[kind], rt.at[kind, q, half_s], ag_s.at[3 + kind], rt_r.at[kind, q, half_s],
                   at(l, y, oh, x, oc)).wait_send()


def local(snapshots, var_index, modes, retained):
    rows, cols = snapshots.shape
    n_space, n_time = lax.axis_size("space"), lax.axis_size("tm")
    total_rows = rows * n_space
    count = float(total_rows // VARS * (cols * n_time))
    root = float(total_rows) ** 0.5
    r = modes.shape[1]
    fk = (rows // 128 + 1) // 2 * 128
    dma = pltpu.SemaphoreType.DMA

    def body(*refs):
        kernel(count, root, fk, *refs)

    vmem = pl.BlockSpec(memory_space=pltpu.VMEM)
    return pl.pallas_call(
        body,
        name="gram",
        out_shape=(jax.ShapeDtypeStruct((cols * n_time, cols), F32), jax.ShapeDtypeStruct((r // n_space, cols), F32)),
        in_specs=[vmem, vmem, vmem, pl.BlockSpec(memory_space=pltpu.SMEM)],
        out_specs=(vmem, vmem),
        scratch_shapes=[
            pltpu.VMEM((cols, rows), BF16),
            pltpu.VMEM((3, cols, rows), BF16),
            pltpu.VMEM((cols, rows), BF16),
            pltpu.VMEM((cols, fk), BF16),
            pltpu.VMEM((cols, fk), BF16),
            pltpu.VMEM((4, cols, rows), BF16),
            pltpu.VMEM((cols, rows), BF16),
            pltpu.VMEM((cols, fk), BF16),
            pltpu.VMEM((VARS, rows), F32),
            pltpu.VMEM((1, rows), F32),
            pltpu.VMEM((1, rows), F32),
            pltpu.VMEM((r, rows), BF16),
            pltpu.VMEM((24, 128), F32),
            pltpu.VMEM((24, 128), F32),
            pltpu.VMEM((7, 24, 128), F32),
            pltpu.VMEM((15, 24, 128), F32),
            pltpu.VMEM((3, 4 * cols, cols), F32),
            pltpu.VMEM((8, 3, 128, cols), BF16),
            pltpu.VMEM((7, 3, 128, cols), BF16),
            pltpu.VMEM((r, cols), F32),
            pltpu.VMEM((7, 8, cols), F32),
            pltpu.VMEM((3, 128, cols), BF16),
            pltpu.VMEM((2, cols, 128), BF16),
            pltpu.VMEM((3, 8, 128, cols), BF16),
            pltpu.VMEM((2, 4, 2, cols, 128), BF16),
            dma((8,)), dma((8,)), dma((7,)), dma((7,)), dma((15,)), dma((15,)),
            dma((7,)), dma((7,)), dma((7,)), dma((7,)), dma((40,)), dma((3, 8)), dma((2, 4, 2)),
        ],
        compiler_params=pltpu.CompilerParams(
            collective_id=0, has_side_effects=True, vmem_limit_bytes=60 * 2 ** 20),
    )(snapshots, var_index.reshape(1, rows), modes, retained)


def solution(mesh):
    return jax.shard_map(
        local,
        mesh=mesh,
        in_specs=(P("space", "tm"), P("space"), P("space", None), P()),
        out_specs=(P(None, "tm"), P("space", "tm")),
        check_vma=False,
    )
```

time: 480 us -> 145 us (0.30)
  waiting for transfers between devices: 299 us -> 0 us
  Pallas kernels: 0 us -> 133 us
  blocking collectives: 131 us -> 0 us
  matrix products: 15.5 us -> 0 us
  other arithmetic: 13.8 us -> 0 us
  between operations: 14.6 us -> 1.29 us
  local copies, waits for them, and re-layouts: 0.65 us -> 8.62 us
    all_gather x1 -> x0, waiting for transfers between devices: 170 us -> none  [local(): lax.all_gather(scaled, 'tm', axis=1, tiled=True)]
    pallas_call x0 -> x1, Pallas kernels: none -> 133 us  [local(): pl.pallas_call(body, name='gram', out_shape=(jax.ShapeDtypeStruct((cols *...]
    psum x2 -> x0, blocking collectives: 131 us -> none  [the longest x1 68.7 us: local(): sums = lax.psum(jnp.sum(onehot * row_sum[:, None], axis=0), ('space', 'tm'))]
    psum x1 -> x0, waiting for transfers between devices: 100 us -> none  [space_total(): return lax.psum(partial_value, 'space')]
    reduce_scatter x1 -> x0, waiting for transfers between devices: 28.7 us -> none  [local(): lax.psum_scatter(cross(kept, scaled), 'space', scatter_dimension=0, tiled...]
    dot_general x2 -> x0, matrix products: 15.5 us -> none  [cross(): lax.dot_general(left, right, (((0,), (0,)), ((), ())), preferred_element_...]
    unnamed x8 -> x5, local copies, waits for them, and re-layouts: 0.65 us -> 7.28 us
    reduce_sum x6 -> x0, other arithmetic: 6.37 us -> none  [the longest x1 2.39 us: local(): row_sq = jnp.sum(centered * centered, axis=1)]
  transfers between devices with their start and end apart: 3 -> 0, of which waited for: 3 -> 0; matrix products, arithmetic and copies ran while one was open for 1% -> 0% of each run, Pallas kernels for 0% -> 0%
where the time goes in v1:
time: 145 us; the launch traced here: 143 us
  Pallas kernels  133 us (92%)
  local copies, waits for them, and re-layouts  8.62 us (6%)
    pallas_call x1, Pallas kernels, local(): pl.pallas_call(body, name='gram', out_shape=(jax.ShapeDtypeStruct((cols *...  133 us
    unnamed x5, local copies, waits for them, and re-layouts  7.28 us

profile of v1, /device:TPU:1, one launch (start us, length us, event | category | flops | bytes accessed | tf_op | source)
XLA Modules:
  0.0 142.6 jit_solution(16876587515335622808)
XLA Ops:
  1.3 1.3 reshape.7.refs_1_
  2.6 2.2 %copy.6.refs_2_ = bf16[3200,64]{1,0:T(8,128)(2,1)} copy(bf16[3200,64]{0,1:T(8,128)(2,1)} %param.6) | data formatting | bytes 819200 | tf_op args[2]
  4.8 132.7 %gram.1 = (f32[4096,256]{1,0:T(8,128)}, f32[8,256]{1,0:T(8,128)}) custom-call(bf16[3200,256]{1,0:T(8,128)(2,1)} %refs_0_.1, s32[1,3200]{1,0:T(1,128)} %reshape.7.refs_1_, bf16[3200,64]{1,0:T(8,128)(2,1)} %copy.6.refs_2_, s32[1]{0:T(128)S(6)} %copy.9.refs_3_), custom_call_target="tpu_custom_call" | custom-call | tf_op jit(solution)/shard_map/gram/pallas_call | solution.py:302
  137.5 0.0 copy-start
  137.5 4.5 %copy.10 = f32[4096,256]{1,0:T(8,128)} copy(f32[4096,256]{1,0:T(8,128)} %get-tuple-element.4) | data formatting | bytes 8388608
  142.0 0.0 copy-done
  142.0 0.6 copy.11
Async XLA Ops:
  137.5 4.5 %copy-start = (f32[8,256]{1,0:T(8,128)S(1)}, f32[8,256]{1,0:T(8,128)}, u32[]{:S(2)}) copy-start(f32[8,256]{1,0:T(8,128)} %get-tuple-element.5) | copy-start | bytes 24580

commit v2 on v1

--- a/solution.py
+++ b/solution.py
@@ -36,9 +36,9 @@
     return n, total, squares
 
 
-def kernel(count, root, fk, x_ref, vi_ref, modes_ref, ret_ref, gram_ref, red_ref,
+def kernel(count, root, fk, x_ref, vi_ref, modes_ref, ret_ref, ra, rt, red_ref,
            xt, raw, rawe, relay, rawf, sc, sce, scf, hot, mean_l, inv_l, kept,
-           tile1, tile2, got1, got2, part, cs, rs, redp, redr, piece, pieceT, ra, rt,
+           tile1, tile2, got1, got2, part, cs, rs, redp, redr, piece, pieceT,
            bulk_s, bulk_r, st1_s, st1_r, st2_s, st2_r, rs_s, rs_r, rd_s, rd_r, ag_s, ra_r, rt_r):
     l, y, h, x, c = place()
     s = l * NY + y
@@ -71,19 +71,26 @@
         return pltpu.make_async_remote_copy(src, dst, ss, rsem, device_id=dev, device_id_type=MESH)
 
     fs_mine = pl.multiple_of((x // 2) * (rows - fk), 128)
-    half = cols // 2
-    to_f = [remote(xt.at[pl.ds(half * k, half), pl.ds(fs_mine, fk)], relay.at[pl.ds(half * k, half)],
-                   bulk_s.at[k], bulk_r.at[k], at(l, y, h, (x + NX - 1) % NX, c)) for k in range(2)]
-    to_e = remote(xt, rawe, bulk_s.at[2], bulk_r.at[2], at(l, y, h, (x + 1) % NX, c))
-    to_z = remote(xt, raw.at[1], bulk_s.at[3], bulk_r.at[3], at(l, y, 1 - h, x, c))
-    to_core = remote(xt, raw.at[0], bulk_s.at[4], bulk_r.at[4], at(l, y, h, x, 1 - c))
-    for cp in to_f:
-        cp.start()
-    to_e.start()
-    to_z.start()
-    to_core.start()
-
-    hot[...] = (vi_ref[...] == lax.broadcasted_iota(jnp.int32, (VARS, rows), 0)).astype(F32)
+    cuts = [0, 32, 128, cols]
+    parts = [pl.ds(lo, hi - lo) for lo, hi in zip(cuts, cuts[1:])]
+    to_f, to_e, to_z, to_core, to_diag, fwd = [], [], [], [], [], []
+    for k, r in enumerate(parts):
+        left = at(l, y, h, (x + NX - 1) % NX, c)
+        core = at(l, y, h, x, 1 - c)
+        to_f.append(remote(xt.at[r, pl.ds(fs_mine, fk)], relay.at[r], bulk_s.at[0, k], bulk_r.at[0, k], left))
+        to_e.append(remote(xt.at[r], rawe.at[r], bulk_s.at[1, k], bulk_r.at[1, k], at(l, y, h, (x + 1) % NX, c)))
+        to_z.append(remote(xt.at[r], raw.at[1, r], bulk_s.at[2, k], bulk_r.at[2, k], at(l, y, 1 - h, x, c)))
+        to_core.append(remote(xt.at[r], raw.at[0, r], bulk_s.at[3, k], bulk_r.at[3, k], core))
+        to_diag.append(remote(raw.at[1, r], raw.at[2, r], bulk_s.at[4, k], bulk_r.at[4, k], core))
+        fwd.append(remote(relay.at[r], rawf.at[r], bulk_s.at[5, k], bulk_r.at[5, k], left))
+
+    def send_part(k):
+        for cp in (to_f[k], to_e[k], to_z[k], to_core[k]):
+            cp.start()
+
+    send_part(0)
+
+    hot[...] = (vi_ref[...][None, :] == lax.broadcasted_iota(jnp.int32, (VARS, rows), 0)).astype(F32)
 
     def colsum(fn):
         def body(k, acc):
@@ -110,10 +117,9 @@
     sends1 = [remote(tile1, got1.at[i], st1_s.at[i], st1_r.at[i], dev1(*d)) for i, d in enumerate(ring1)]
     for cp in sends1:
         cp.start()
-    for k in range(ntile):
-        kept[:, 128 * k:128 * k + 128] = modes_ref[128 * k:128 * k + 128, :].T
+    send_part(1)
     keep = lax.broadcasted_iota(jnp.int32, kept.shape, 0) < ret_ref[0]
-    kept[...] = jnp.where(keep, kept[...].astype(F32), 0.0).astype(BF16)
+    kept[...] = jnp.where(keep, modes_ref[...].astype(F32), 0.0).astype(BF16)
     for cp in sends1:
         cp.wait_recv()
     n2, sum2, sq2 = merge([tile1[...]] + [got1[i] for i in range(len(ring1))])
@@ -123,6 +129,7 @@
     sends2 = [remote(tile2, got2.at[i], st2_s.at[i], st2_r.at[i], dev2(*d)) for i, d in enumerate(ring2)]
     for cp in sends2:
         cp.start()
+    send_part(2)
     for cp in sends2:
         cp.wait_recv()
     _, sum3, sq3 = merge([tile2[...]] + [got2[i] for i in range(len(ring2))])
@@ -131,56 +138,59 @@
     mean_l[...] = jnp.sum(hot[...] * mean[:, 0:1], axis=0, keepdims=True)
     inv_l[...] = jnp.sum(hot[...] * inv[:, 0:1], axis=0, keepdims=True)
 
-    def scale_to(dst, src):
+    def scale_to(dst, src, lo, n, m, v):
         def body(k, _):
-            r = pl.ds(pl.multiple_of(k * 16, 16), 16)
-            dst[r, :] = ((src[r, :].astype(F32) - mean_l[...]) * inv_l[...]).astype(BF16)
+            r = pl.ds(pl.multiple_of(lo + k * 16, 16), 16)
+            dst[r, :] = ((src[r, :].astype(F32) - m) * v).astype(BF16)
             return 0
-        lax.fori_loop(0, cols // 16, body, 0)
-
-    scale_to(sc.at[q], xt)
-    redp[...] = nt(kept[...], sc[q])
-
-    fwd = [remote(relay.at[pl.ds(half * k, half)], rawf.at[pl.ds(half * k, half)],
-                  bulk_s.at[5 + k], bulk_r.at[5 + k], at(l, y, h, (x + NX - 1) % NX, c)) for k in range(2)]
-    to_core.wait_recv()
-    scale_to(sc.at[h * 2 + (1 - c)], raw.at[0])
-    for k in range(2):
-        to_f[k].wait_recv()
-        fwd[k].start()
-    to_z.wait_recv()
-    to_diag = remote(raw.at[1], raw.at[2], bulk_s.at[7], bulk_r.at[7], at(l, y, h, x, 1 - c))
-    to_diag.start()
-    scale_to(sc.at[(1 - h) * 2 + c], raw.at[1])
-    to_e.wait_recv()
-    scale_to(sce, rawe)
-    to_diag.wait_recv()
-    scale_to(sc.at[(1 - h) * 2 + (1 - c)], raw.at[2])
-
-    def product(kind, right, lanes):
-        def body(i, _):
-            part[kind, pl.ds(pl.multiple_of(i * cols, cols), cols), :] = nt(sc[i, :, lanes], right)
-            return 0
-        lax.fori_loop(0, 4, body, 0)
-
-    product(0, sc[q], slice(None))
-    product(1, sce[...], slice(None))
-
-    for k in range(2):
-        fwd[k].wait_recv()
+        lax.fori_loop(0, n // 16, body, 0)
+
+    def scale(dst, src, lo=0, n=cols):
+        scale_to(dst, src, lo, n, mean_l[...], inv_l[...])
+
     fs = pl.multiple_of((((x + 2) % NX) // 2) * (rows - fk), 128)
     fl = pl.ds(fs, fk)
     over = 2 * fk - rows
     first = lax.broadcasted_iota(jnp.int32, (1, fk), 1) < over
     drop = jnp.logical_and(first, x < 2)
+    f_mean = mean_l[:, fl]
     f_inv = jnp.where(drop, 0.0, inv_l[:, fl])
 
-    def fbody(k, _):
-        r = pl.ds(pl.multiple_of(k * 16, 16), 16)
-        scf[r, :] = ((rawf[r, :].astype(F32) - mean_l[:, fl]) * f_inv).astype(BF16)
-        return 0
-    lax.fori_loop(0, cols // 16, fbody, 0)
-    product(2, scf[...], fl)
+    def product(kind, i, right, lanes):
+        part[kind, pl.ds(pl.multiple_of(i * cols, cols), cols), :] = nt(sc[i, :, lanes], right)
+
+    every = slice(None)
+    q1, q2, q3 = h * 2 + (1 - c), (1 - h) * 2 + c, (1 - h) * 2 + (1 - c)
+    scale(sc.at[q], xt)
+    redp[...] = nt(kept[...], sc[q])
+    product(0, q, sc[q], every)
+    for k in range(len(parts)):
+        to_core[k].wait_recv()
+    scale(sc.at[q1], raw.at[0])
+    product(0, q1, sc[q], every)
+
+    for k in range(len(parts)):
+        lo, n = cuts[k], cuts[k + 1] - cuts[k]
+        to_f[k].wait_recv()
+        fwd[k].start()
+        to_z[k].wait_recv()
+        to_diag[k].start()
+        scale(sc.at[q2], raw.at[1], lo, n)
+        to_e[k].wait_recv()
+        scale(sce, rawe, lo, n)
+        to_diag[k].wait_recv()
+        scale(sc.at[q3], raw.at[2], lo, n)
+        if k > 0:
+            fwd[k - 1].wait_recv()
+            scale_to(scf, rawf, cuts[k - 1], cuts[k] - cuts[k - 1], f_mean, f_inv)
+    product(0, q2, sc[q], every)
+    product(0, q3, sc[q], every)
+    for i in range(4):
+        product(1, i, sce[...], every)
+    fwd[-1].wait_recv()
+    scale_to(scf, rawf, cuts[-2], cuts[-1] - cuts[-2], f_mean, f_inv)
+    for i in range(4):
+        product(2, i, scf[...], fl)
 
     ring3 = [(dl, dy) for dl in range(2) for dy in range(NY) if (dl, dy) != (0, 0)]
     for i in range(NSPACE):
@@ -239,7 +249,8 @@
                 else:
                     cp.start()
                     agsend.append(cp)
-    ra[0, s] = piece[0]
+    mine = pltpu.make_async_copy(piece.at[0], ra.at[0, s], ra_r.at[0, s])
+    mine.start()
 
     for a in dsend:
         a.wait_recv()
@@ -251,38 +262,44 @@
     def got(ref, sem):
         pltpu.make_async_copy(ref, ref, sem).wait()
 
-    def rows_of(hc, xx):
-        return ((hc // 2) * 8 + xx * 2 + hc % 2) * cols
-
     for kind in range(3):
-        xx = [x, (x + 1) % NX, (x + 2) % NX][kind]
         for j in range(NSPACE):
-            if kind == 0:
-                @pl.when(s != j)
-                def _():
-                    got(ra.at[0, j], ra_r.at[0, j])
-            else:
-                got(ra.at[kind, j], ra_r.at[kind, j])
-            r0 = pl.multiple_of(rows_of(j // 2, xx) + (j % 2) * 128, 128)
-            gram_ref[pl.ds(r0, 128), :] = ra[kind, j].astype(F32)
+            got(ra.at[kind, j], ra_r.at[kind, j])
     for kind in range(2):
-        xx = [(x + NX - 1) % NX, (x + 2) % NX][kind]
         for hc in range(4):
-            r0 = pl.multiple_of(rows_of(hc, xx), cols)
             for b in range(2):
                 got(rt.at[kind, hc, b], rt_r.at[kind, hc, b])
-                val = rt[kind, hc, b].astype(F32)
-                if kind == 1:
-                    val = val + gram_ref[pl.ds(r0, cols), 128 * b:128 * b + 128]
-                gram_ref[pl.ds(r0, cols), 128 * b:128 * b + 128] = val
-
-    for cp in to_f + fwd + [to_e, to_z, to_core, to_diag] + sends1 + sends2 + rsend + dsend + agsend:
+
+    for cp in to_f + fwd + to_e + to_z + to_core + to_diag + sends1 + sends2 + rsend + dsend + agsend:
         cp.wait_send()
     for kind in range(2):
         @pl.when(own != q)
         def _():
             remote(pieceT.at[kind], rt.at[kind, q, half_s], ag_s.at[3 + kind], rt_r.at[kind, q, half_s],
                    at(l, y, oh, x, oc)).wait_send()
+
+
+def assemble(x_ref, ra, rt, red_in, gram_ref, red_ref):
+    k = pl.program_id(0)
+    red_ref[...] = red_in[...]
+    cols = gram_ref.shape[3]
+    for kind in range(3):
+        @pl.when(k == kind)
+        def _():
+            for j in range(NSPACE):
+                rows = pl.ds((j % 4) * 128, 128)
+                gram_ref[j // 4, 0, rows, :] = ra[kind, j].astype(F32)
+    for kind in range(2):
+        @pl.when(k == 3 - kind)
+        def _():
+            for hc in range(4):
+                rows = pl.ds((hc % 2) * cols, cols)
+                for b in range(2):
+                    lanes = pl.ds(128 * b, 128)
+                    val = rt[kind, hc, b].astype(F32)
+                    if kind == 1:
+                        val = val + gram_ref[hc // 2, 0, rows, lanes]
+                    gram_ref[hc // 2, 0, rows, lanes] = val
 
 
 def local(snapshots, var_index, modes, retained):
@@ -299,12 +316,13 @@
         kernel(count, root, fk, *refs)
 
     vmem = pl.BlockSpec(memory_space=pltpu.VMEM)
-    return pl.pallas_call(
+    ra, rt, red = pl.pallas_call(
         body,
         name="gram",
-        out_shape=(jax.ShapeDtypeStruct((cols * n_time, cols), F32), jax.ShapeDtypeStruct((r // n_space, cols), F32)),
+        out_shape=(jax.ShapeDtypeStruct((3, 8, 128, cols), BF16), jax.ShapeDtypeStruct((2, 4, 2, cols, 128), BF16),
+                   jax.ShapeDtypeStruct((r // n_space, cols), F32)),
         in_specs=[vmem, vmem, vmem, pl.BlockSpec(memory_space=pltpu.SMEM)],
-        out_specs=(vmem, vmem),
+        out_specs=(pl.BlockSpec(memory_space=pl.ANY), pl.BlockSpec(memory_space=pl.ANY), vmem),
         scratch_shapes=[
             pltpu.VMEM((cols, rows), BF16),
             pltpu.VMEM((3, cols, rows), BF16),
@@ -329,14 +347,28 @@
             pltpu.VMEM((7, 8, cols), F32),
             pltpu.VMEM((3, 128, cols), BF16),
             pltpu.VMEM((2, cols, 128), BF16),
-            pltpu.VMEM((3, 8, 128, cols), BF16),
-            pltpu.VMEM((2, 4, 2, cols, 128), BF16),
-            dma((8,)), dma((8,)), dma((7,)), dma((7,)), dma((15,)), dma((15,)),
+            dma((6, 3)), dma((6, 3)), dma((7,)), dma((7,)), dma((15,)), dma((15,)),
             dma((7,)), dma((7,)), dma((7,)), dma((7,)), dma((40,)), dma((3, 8)), dma((2, 4, 2)),
         ],
         compiler_params=pltpu.CompilerParams(
             collective_id=0, has_side_effects=True, vmem_limit_bytes=60 * 2 ** 20),
-    )(snapshots, var_index.reshape(1, rows), modes, retained)
+    )(snapshots, var_index, modes.T, retained)
+    x = ((lax.axis_index("tm") // 2) % NX).reshape(1)
+    gram, red = pl.pallas_call(
+        assemble,
+        name="columns",
+        grid_spec=pltpu.PrefetchScalarGridSpec(
+            num_scalar_prefetch=1,
+            grid=(NX,),
+            in_specs=[pl.BlockSpec(ra.shape, lambda k, x: (0,) * 4), pl.BlockSpec(rt.shape, lambda k, x: (0,) * 5),
+                      pl.BlockSpec(red.shape, lambda k, x: (0, 0))],
+            out_specs=[pl.BlockSpec((2, 1, 2 * cols, cols), lambda k, x: (0, (x[0] + k) % NX, 0, 0)),
+                       pl.BlockSpec(red.shape, lambda k, x: (0, 0))],
+        ),
+        out_shape=(jax.ShapeDtypeStruct((2, NX, 2 * cols, cols), F32), jax.ShapeDtypeStruct(red.shape, F32)),
+        compiler_params=pltpu.CompilerParams(vmem_limit_bytes=32 * 2 ** 20),
+    )(x, ra, rt, red)
+    return gram.reshape(cols * n_time, cols), red
 
 
 def solution(mesh):

time: 145 us -> 126 us (0.87)
  the two profiles are of different devices: /device:TPU:1 before, /device:TPU:54 now
where the time goes in v2:
time: 126 us; the launch traced here: 125 us
  Pallas kernels  121 us (96%)
  local copies, waits for them, and re-layouts  3.32 us (3%)
  between operations  1.32 us (1%)
    pallas_call x1, Pallas kernels, local(): pl.pallas_call(body, name='gram', out_shape=(jax.ShapeDtypeStruct((3, 8,...  118 us
    unnamed x6, local copies, waits for them, and re-layouts  3.32 us
    pallas_call x1, Pallas kernels, local(): pl.pallas_call(assemble, name='columns', grid_spec=pltpu.PrefetchScalarGr...  2.54 us

profile of v2, /device:TPU:54, one launch (start us, length us, event | category | flops | bytes accessed | tf_op | source)
XLA Modules:
  0.0 125.3 jit_solution(8715092388694145910)
XLA Ops:
  1.3 118.1 %gram.1 = (bf16[3,8,128,256]{3,2,1,0:T(8,128)(2,1)}, bf16[2,4,2,256,128]{4,3,2,1,0:T(8,128)(2,1)}, f32[8,256]{1,0:T(8,128)}) custom-call(bf16[3200,256]{1,0:T(8,128)(2,1)} %refs_0_.1, s32[3200]{0:T(1024)} %refs_1_.1, bf16[64,3200]{1,0:T(8,128)(2,1)} %bitcast.3, s32[1]{0:T(128)S(6)} %copy.6.refs_3_), custom_call_target="tpu_custom_call" | custom-call | tf_op jit(solution)/shard_map/gram/pallas_call | solution.py:319
  119.4 0.0 copy-start
  119.4 1.4 %copy-done = bf16[3,8,128,256]{3,2,1,0:T(8,128)(2,1)S(1)} copy-done((bf16[3,8,128,256]{3,2,1,0:T(8,128)(2,1)S(1)}, bf16[3,8,128,256]{3,2,1,0:T(8,128)(2,1)}, u32[]{:S(2)}) %copy-start) | copy-done | bytes 1572888
  120.8 0.0 copy-start.1
  120.8 1.2 copy-done.1
  122.0 0.0 copy-start.2
  122.0 0.7 copy-done.2
  122.7 2.5 %columns.1 = (f32[2,4,512,256]{3,2,1,0:T(8,128)}, f32[8,256]{1,0:T(8,128)}) custom-call(s32[1]{0:T(128)} %bitcast.x_ref, bf16[3,8,128,256]{3,2,1,0:T(8,128)(2,1)S(1)} %copy-done, bf16[2,4,2,256,128]{4,3,2,1,0:T(8,128)(2,1)S(1)} %copy-done.1, f32[8,256]{1,0:T(8,128)S(1)} %copy-done.2), custom_call_target="tpu_custom_call" | custom-call | tf_op jit(solution)/shard_map/columns/pallas_call | solution.py:357
Async XLA Ops:
  119.4 1.4 %copy-start = (bf16[3,8,128,256]{3,2,1,0:T(8,128)(2,1)S(1)}, bf16[3,8,128,256]{3,2,1,0:T(8,128)(2,1)}, u32[]{:S(2)}) copy-start(bf16[3,8,128,256]{3,2,1,0:T(8,128)(2,1)} %get-tuple-element.7.ra) | copy-start | bytes 4718596
  120.8 1.2 copy-start.1
  122.0 0.7 copy-start.2

commit v3 on v2

v3 whole, which is shorter than its diff:
```python
import jax
import jax.numpy as jnp
from jax import lax
from jax.experimental import pallas as pl
from jax.experimental.pallas import tpu as pltpu
from jax.sharding import PartitionSpec as P

MESH = pl.DeviceIdType.MESH
VARS = 8
NY, NX = 4, 4
F32, BF16 = jnp.float32, jnp.bfloat16


def place():
    s, t = lax.axis_index("space"), lax.axis_index("tm")
    return s // NY, s % NY, t // 8, (t // 2) % NX, t % 2


def at(l, y, h, x, c):
    return (l * NY + y, h * 8 + x * 2 + c)


def nt(a, b):
    return lax.dot_general(a, b, (((1,), (1,)), ((), ())), preferred_element_type=F32)


def merge(tiles):
    n = sum(t[0:8] for t in tiles)
    total = sum(t[8:16] for t in tiles)
    mean = total / jnp.maximum(n, 1.0)
    squares = jnp.zeros_like(n)
    for t in tiles:
        off = t[8:16] / jnp.maximum(t[0:8], 1.0) - mean
        squares = squares + t[16:24] + t[0:8] * off * off
    return n, total, squares


def role(g, y):
    two, odd = y // 2, y % 2
    if g == 0:
        return 0, 0, two, odd
    if g in (1, 3):
        return 0, 1 + odd, two, g // 2
    if g == 4:
        return 1, 1 + odd, two, 1 - two
    last = g // 3
    return (1, 0, last, odd) if two == 0 else (1, 1 + odd, last, last)


SETS = 6
MIXED = (2, 5)
EARLY = 3
YFIRST = (3, 5)
CUTS = (0, 32, 128, 160, 192, 224, 256)
ZCUTS = (0, 64, 128, 160, 192, 224, 256)


def kernel(count, root, fk, x_ref, vi_ref, modes_ref, ret_ref, fin, red_ref,
           xt, raw, rawe, relay, rawf, near, far, ef, hot, mean_l, inv_l, kept,
           tile1, tile2, got1, got2, ps, cs, rs, tmp, r2, redp, redr, pc, pt,
           bulk_s, bulk_r, st1_s, st1_r, st2_s, st2_r, rs_s, rs_r, r2_s, r2_r, rd_s, rd_r, a_s, fin_r, b_s, b_r,
           ay_s, al_s, late_r, rd, d_s, d_r):
    l, y, h, x, c = place()
    s = l * NY + y
    rows = xt.shape[1]
    cols = xt.shape[0]
    ntile = rows // 128
    drain = []

    ring1 = [(dx, dc) for dx in range(NX) for dc in range(2) if (dx, dc) != (0, 0)]
    ring2 = [(dy, dl, dh) for dy in range(NY) for dl in range(2) for dh in range(2) if (dy, dl, dh) != (0, 0, 0)]

    def dev1(dx, dc):
        return at(l, y, h, (x + dx) % NX, (c + dc) % 2)

    def dev2(dy, dl, dh):
        return at((l + dl) % 2, (y + dy) % NY, (h + dh) % 2, x, c)

    barrier = pltpu.get_barrier_semaphore()
    for d in ring1:
        pl.semaphore_signal(barrier, inc=1, device_id=dev1(*d), device_id_type=MESH)
    for d in ring2:
        pl.semaphore_signal(barrier, inc=1, device_id=dev2(*d), device_id_type=MESH)

    def turn(half):
        for k in range(ntile):
            xt[128 * half:128 * half + 128, 128 * k:128 * k + 128] = x_ref[128 * k:128 * k + 128, 128 * half:128 * half + 128].T

    turn(0)
    pl.semaphore_wait(barrier, len(ring1) + len(ring2))

    def remote(src, dst, ss, rsem, dev):
        return pltpu.make_async_remote_copy(src, dst, ss, rsem, device_id=dev, device_id_type=MESH)

    def go(*copies):
        for cp in copies:
            cp.start()
            drain.append(cp)

    fs_mine = pl.multiple_of((x // 2) * (rows - fk), 128)
    parts = [pl.ds(lo, hi - lo) for lo, hi in zip(CUTS, CUTS[1:])]
    to_f, to_e, to_z, to_core, to_diag, fwd = [], [], [], [], [], []
    left, core = at(l, y, h, (x + NX - 1) % NX, c), at(l, y, h, x, 1 - c)
    for k, r in enumerate(parts):
        to_f.append(remote(xt.at[r, pl.ds(fs_mine, fk)], relay.at[r], bulk_s.at[0, k], bulk_r.at[0, k], left))
        to_e.append(remote(xt.at[r], rawe.at[r], bulk_s.at[1, k], bulk_r.at[1, k], at(l, y, h, (x + 1) % NX, c)))
        fwd.append(remote(relay.at[r], rawf.at[r], bulk_s.at[5, k], bulk_r.at[5, k], left))
    for k, r in enumerate([pl.ds(lo, hi - lo) for lo, hi in zip(ZCUTS, ZCUTS[1:])]):
        to_z.append(remote(xt.at[r], raw.at[1, r], bulk_s.at[2, k], bulk_r.at[2, k], at(l, y, 1 - h, x, c)))
        to_diag.append(remote(raw.at[1, r], raw.at[2, r], bulk_s.at[4, k], bulk_r.at[4, k], core))
    to_core = remote(xt, raw.at[0], bulk_s.at[3, 0], bulk_r.at[3, 0], core)

    go(to_f[0], to_e[0], to_z[0])
    turn(1)
    go(to_core)

    hot[...] = (vi_ref[...][None, :] == lax.broadcasted_iota(jnp.int32, (VARS, rows), 0)).astype(F32)

    def colsum(fn):
        def body(k, acc):
            blk = xt[pl.ds(pl.multiple_of(k * 16, 16), 16), :].astype(F32)
            return acc + fn(blk)
        acc = lax.fori_loop(0, cols // 16, body, jnp.zeros((16, rows), F32))
        return jnp.sum(acc, axis=0, keepdims=True)

    def wide(v):
        return jnp.broadcast_to(v, (VARS, 128))

    n1 = jnp.sum(hot[...], axis=1, keepdims=True) * cols
    sum1 = jnp.sum(hot[...] * colsum(lambda b: b), axis=1, keepdims=True)
    m1 = sum1 / jnp.maximum(n1, 1.0)
    mean_l[...] = jnp.sum(hot[...] * m1, axis=0, keepdims=True)

    def sq(b):
        d = b - mean_l[...]
        return d * d
    sq1 = jnp.sum(hot[...] * colsum(sq), axis=1, keepdims=True)
    tile1[0:8] = wide(n1)
    tile1[8:16] = wide(sum1)
    tile1[16:24] = wide(sq1)
    sends1 = [remote(tile1, got1.at[i], st1_s.at[i], st1_r.at[i], dev1(*d)) for i, d in enumerate(ring1)]
    go(*sends1)
    go(to_f[1], to_e[1])
    keep = lax.broadcasted_iota(jnp.int32, kept.shape, 0) < ret_ref[0]
    kept[...] = jnp.where(keep, modes_ref[...].astype(F32), 0.0).astype(BF16)
    for half in range(2):
        ef[half, 128:256, :] = jnp.zeros((128, rows), BF16)
    for cp in sends1:
        cp.wait_recv()
    to_f[0].wait_recv()
    go(fwd[0])
    n2, sum2, sq2 = merge([tile1[...]] + [got1[i] for i in range(len(ring1))])
    tile2[0:8] = n2
    tile2[8:16] = sum2
    tile2[16:24] = sq2
    sends2 = [remote(tile2, got2.at[i], st2_s.at[i], st2_r.at[i], dev2(*d)) for i, d in enumerate(ring2)]
    go(*sends2)
    go(to_z[1])
    to_f[1].wait_recv()
    go(fwd[1], to_e[2], *to_f[2:])
    for cp in sends2:
        cp.wait_recv()
    _, sum3, sq3 = merge([tile2[...]] + [got2[i] for i in range(len(ring2))])
    mean = sum3 / count
    inv = 1.0 / jnp.sqrt(sq3 / count + 1e-06)
    mean_l[...] = jnp.sum(hot[...] * mean[:, 0:1], axis=0, keepdims=True)
    inv_l[...] = jnp.sum(hot[...] * inv[:, 0:1], axis=0, keepdims=True)
    go(to_z[2])

    def scale_to(dst, dlo, src, lo, n, m, v):
        def body(k, _):
            a = pl.multiple_of(k * 16, 16)
            dst[pl.ds(dlo + a, 16), :] = ((src[pl.ds(lo + a, 16), :].astype(F32) - m) * v).astype(BF16)
            return 0
        lax.fori_loop(0, n // 16, body, 0)

    def scale(dst, dlo, src, lo, n):
        scale_to(dst, dlo, src, lo, n, mean_l[...], inv_l[...])

    fs = pl.multiple_of((((x + 2) % NX) // 2) * (rows - fk), 128)
    fl = pl.ds(fs, fk)
    over = 2 * fk - rows
    first = lax.broadcasted_iota(jnp.int32, (1, fk), 1) < over
    drop = jnp.logical_and(first, x < 2)

    def scale_f(k):
        half, lo = CUTS[k] // 128, CUTS[k] % 128
        scale_to(ef.at[half, :, fl], 128 + lo, rawf, CUTS[k], CUTS[k + 1] - CUTS[k], mean_l[:, fl],
                 jnp.where(drop, 0.0, inv_l[:, fl]))

    def scale_z(k):
        half, lo, n = ZCUTS[k] // 128, ZCUTS[k] % 128, ZCUTS[k + 1] - ZCUTS[k]
        to_z[k].wait_recv()
        go(to_diag[k])
        scale(far.at[half, c], lo, raw.at[1], ZCUTS[k], n)
        to_diag[k].wait_recv()
        scale(far.at[half, 1 - c], lo, raw.at[2], ZCUTS[k], n)

    def scale_e(k):
        half, lo, n = CUTS[k] // 128, CUTS[k] % 128, CUTS[k + 1] - CUTS[k]
        to_e[k].wait_recv()
        scale(ef.at[half], lo, rawe, CUTS[k], n)

    def near_own():
        for cc in range(2):
            p = nt(near[cc], near[c])
            for k in range(4):
                ps[0, k, cc] = p[128 * (k // 2):128 * (k // 2) + 128, 128 * (k % 2):128 * (k % 2) + 128]

    def near_ef(g, half):
        for cc in range(2):
            p = nt(near[cc], ef[half])
            for k in range(4):
                ps[g, k, cc] = p[128 * (k // 2):128 * (k // 2) + 128, 128 * (k % 2):128 * (k % 2) + 128]

    def far_with(g, slot, ra, right):
        p = nt(far[ra].reshape(256, rows), right)
        for cc in range(2):
            for k in range(2):
                ps[g, slot + k, cc] = p[128 * cc:128 * cc + 128, 128 * k:128 * k + 128]

    def sum_y_start(g):
        cs[g] = ps[g].astype(BF16)
        go(*sum_y[g])

    sum_y = [[remote(cs.at[g, (y + dy) % NY], rs.at[g, dy - 1], rs_s.at[g, dy - 1], rs_r.at[g, dy - 1],
                     at(l, (y + dy) % NY, h, x, c)) for dy in range(1, NY)] for g in range(EARLY)]
    sum_l = [remote(tmp.at[g, 1 - l], r2.at[g], r2_s.at[g], r2_r.at[g], at(1 - l, y, h, x, c)) for g in range(EARLY)]

    ring3 = [(dl, dy) for dl in range(2) for dy in range(NY) if (dl, dy) != (0, 0)]
    sum_s = {}
    for g in range(EARLY, SETS):
        sum_s[g] = [remote(cs.at[g, (y + dy) % NY, (l + dl) % 2], rd.at[g - EARLY, i], d_s.at[g - EARLY, i], d_r.at[g - EARLY, i],
                           at((l + dl) % 2, (y + dy) % NY, h, x, c)) for i, (dl, dy) in enumerate(ring3)]

    def sum_start(g):
        cs[g] = ps[g].astype(BF16)
        go(*sum_s[g])

    def total(g):
        if g < EARLY:
            sum_l[g].wait_recv()
            tot = tmp[g, l] + r2[g]
        else:
            for cp in sum_s[g]:
                cp.wait_recv()
            tot = ps[g, y, l]
            for i in range(len(ring3)):
                tot = tot + rd[g - EARLY, i].astype(F32)
        return tot * (1.0 / root)

    def sum_l_start(g):
        for cp in sum_y[g]:
            cp.wait_recv()
        tot = ps[g, y]
        for k in range(NY - 1):
            tot = tot + rs[g, k].astype(F32)
        tmp[g] = tot
        go(sum_l[g])

    def kinds(g):
        if g == 0:
            return [(None, False)]
        if g in MIXED:
            return [(y < 2, False), (y >= 2, True)]
        return [(None, True)]

    def under(cond, fn):
        if cond is None:
            fn()
        else:
            pl.when(cond)(fn)

    def asis(g, k, two):
        xd = (x + 3 - y % 2) % NX if two else x
        return remote(pc.at[g], fin.at[g, y, l], a_s.at[g, k], fin_r.at[g, l], at((l + k) % 2, y, h, xd, c))

    def turned(g, k):
        hd = (h + role(g, 3)[0]) % 2
        return remote(pt.at[g], fin.at[g, y, 2 + c], a_s.at[g, 2 + k], fin_r.at[g, 2 + c], at((l + k) % 2, y, hd, x, l))

    def publish(g):
        tot = total(g)
        pc[g] = tot.astype(BF16)
        if g > 0:
            pt[g] = tot.T.astype(BF16)
        for cond, two in kinds(g):
            def send(two=two):
                if two:
                    asis(g, 0, True).start()
                    asis(g, 1, True).start()
                    turned(g, 1).start()
                    if role(g, 3)[0]:
                        turned(g, 0).start()
                    else:
                        @pl.when(c == l)
                        def _():
                            pltpu.make_async_copy(pt.at[g], fin.at[g, y, 2 + c], fin_r.at[g, 2 + c]).start()

                        @pl.when(c != l)
                        def _():
                            turned(g, 0).start()
                else:
                    pltpu.make_async_copy(pc.at[g], fin.at[g, y, l], fin_r.at[g, l]).start()
                    asis(g, 1, False).start()
            under(cond, send)

    def along_y(g, dy, n):
        return remote(fin.at[g, y, pl.ds(0, n)], fin.at[g, y, pl.ds(0, n)], b_s.at[g, dy - 1], b_r.at[g, y],
                      at(l, (y + dy) % NY, h, x, c))

    def got(ref, sem):
        pltpu.make_async_copy(ref, ref, sem).wait()

    def spread(g):
        for cond, two in kinds(g):
            def send(two=two):
                n = 4 if two else 2
                for k in range(n):
                    got(fin.at[g, y, k], fin_r.at[g, k])
                for dy in range(1, NY):
                    along_y(g, dy, n).start()
            under(cond, send)

    def finish(g):
        for j in range(NY):
            n = 4 if role(g, j)[1] else 2

            @pl.when(y != j)
            def _():
                got(fin.at[g, j, pl.ds(0, n)], b_r.at[g, j])
        for cond, two in kinds(g):
            def wait(two=two):
                n = 4 if two else 2
                for dy in range(1, NY):
                    along_y(g, dy, n).wait_send()
                if two:
                    asis(g, 0, True).wait_send()
                    asis(g, 1, True).wait_send()
                    turned(g, 1).wait_send()
                    if role(g, 3)[0]:
                        turned(g, 0).wait_send()
                    else:
                        @pl.when(c != l)
                        def _():
                            turned(g, 0).wait_send()
                else:
                    asis(g, 1, False).wait_send()
            under(cond, wait)

    def asis_y(g, dy, two):
        xd = (x + 3 - y % 2) % NX if two else x
        return remote(pc.at[g], fin.at[g, y, l], ay_s.at[g, dy, 0], late_r.at[g, y, l], at(l, (y + dy) % NY, h, xd, c))

    def turned_y(g, dy):
        hd = (h + role(g, 3)[0]) % 2
        return remote(pt.at[g], fin.at[g, y, 2 + c], ay_s.at[g, dy, 1], late_r.at[g, y, 2 + c],
                      at(l, (y + dy) % NY, hd, x, l))

    def publish_late(g):
        tot = total(g)
        pc[g] = tot.astype(BF16)
        pt[g] = tot.T.astype(BF16)
        for cond, two in kinds(g):
            def send(two=two):
                for dy in range(1, NY):
                    asis_y(g, dy, two).start()
                    if two:
                        turned_y(g, dy).start()
                if two:
                    asis_y(g, 0, True).start()
                    if role(g, 3)[0]:
                        turned_y(g, 0).start()
                    else:
                        @pl.when(c == l)
                        def _():
                            pltpu.make_async_copy(pt.at[g], fin.at[g, y, 2 + c], late_r.at[g, y, 2 + c]).start()

                        @pl.when(c != l)
                        def _():
                            turned_y(g, 0).start()
                else:
                    pltpu.make_async_copy(pc.at[g], fin.at[g, y, l], late_r.at[g, y, l]).start()
            under(cond, send)

    def across_asis(g, j):
        return remote(fin.at[g, j, l], fin.at[g, j, l], al_s.at[g, j, 0], late_r.at[g, j, l], at(1 - l, y, h, x, c))

    def across_turned(g, j):
        pair = fin.at[g, j, pl.ds(2, 2)]
        return remote(pair, pair, al_s.at[g, j, 1], late_r.at[g, j, 2], at(1 - l, y, h, x, c))

    def spread_late(g):
        for j in range(NY):
            got(fin.at[g, j, l], late_r.at[g, j, l])
            across_asis(g, j).start()
        for j in range(NY):
            if role(g, j)[1]:
                @pl.when(c == l)
                def _():
                    for k in (2, 3):
                        got(fin.at[g, j, k], late_r.at[g, j, k])
                    across_turned(g, j).start()

    def finish_late(g):
        for j in range(NY):
            got(fin.at[g, j, 1 - l], late_r.at[g, j, 1 - l])
            across_asis(g, j).wait_send()
            if role(g, j)[1]:
                @pl.when(c != l)
                def _():
                    got(fin.at[g, j, pl.ds(2, 2)], late_r.at[g, j, 2])

                @pl.when(c == l)
                def _():
                    across_turned(g, j).wait_send()
        for cond, two in kinds(g):
            def wait(two=two):
                for dy in range(1, NY):
                    asis_y(g, dy, two).wait_send()
                    if two:
                        turned_y(g, dy).wait_send()
                if two:
                    asis_y(g, 0, True).wait_send()
                    if role(g, 3)[0]:
                        turned_y(g, 0).wait_send()
                    else:
                        @pl.when(c != l)
                        def _():
                            turned_y(g, 0).wait_send()
            under(cond, wait)

    scale(near.at[c], 0, xt, 0, cols)
    to_core.wait_recv()
    scale(near.at[1 - c], 0, raw.at[0], 0, cols)
    near_own()
    sum_y_start(0)
    redp[...] = nt(kept[...], near[c])
    dsend = []
    for i, (dl, dy) in enumerate(ring3):
        tl, ty = (l + dl) % 2, (y + dy) % NY
        dsend.append(remote(redp.at[pl.ds(pl.multiple_of((tl * NY + ty) * 8, 8), 8)], redr.at[i], rd_s.at[i], rd_r.at[i],
                            at(tl, ty, h, x, c)))
    go(*dsend)
    scale_e(0)
    scale_z(0)
    sum_l_start(0)
    scale_z(1)
    go(to_e[3], to_z[3])
    far_with(2, 0, 0, near[c])
    scale_e(1)
    for k in range(2):
        fwd[k].wait_recv()
        scale_f(k)
    near_ef(1, 0)
    sum_y_start(1)
    far_with(2, 2, 0, ef[0])
    sum_y_start(2)
    publish(0)
    to_f[2].wait_recv()
    go(fwd[2])
    scale_z(2)
    scale_e(2)
    sum_l_start(1)
    sum_l_start(2)
    go(to_e[4], to_z[4])
    to_f[3].wait_recv()
    go(fwd[3])
    scale_z(3)
    scale_e(3)
    spread(0)
    publish(1)
    publish(2)
    go(to_e[5], to_z[5])
    for k in (4, 5):
        to_f[k].wait_recv()
        go(fwd[k])
    for k in (2, 3):
        fwd[k].wait_recv()
        scale_f(k)
    scale_z(4)
    scale_e(4)
    spread(1)
    spread(2)
    scale_z(5)
    far_with(4, 2, 1, ef[0])
    far_with(5, 0, 1, near[c])
    scale_e(5)
    for k in (4, 5):
        fwd[k].wait_recv()
        scale_f(k)
    near_ef(3, 1)
    sum_start(3)
    far_with(4, 0, 0, ef[1])
    sum_start(4)
    far_with(5, 2, 1, ef[1])
    sum_start(5)
    publish_late(3)
    publish(4)
    spread_late(3)
    publish_late(5)
    spread(4)
    spread_late(5)
    for a in dsend:
        a.wait_recv()
    tot = redp[pl.ds(pl.multiple_of(s * 8, 8), 8), :]
    for i in range(len(ring3)):
        tot = tot + redr[i]
    red_ref[...] = tot
    for g in range(SETS):
        (finish_late if g in YFIRST else finish)(g)

    for cp in drain:
        cp.wait_send()


def assemble(place_ref, fin, red_in, gram_ref, red_ref):
    k = pl.program_id(0)
    h = place_ref[1]
    red_ref[...] = red_in[...]

    def tile(nf, block, row, col):
        return (h + nf) % 2, 0, pl.ds(block * 256 + row * 128, 128), pl.ds(col * 128, 128)

    for step in range(NX):
        @pl.when(k == step)
        def _():
            for g in range(SETS):
                for y in range(NY):
                    nf, kind, ra, cb = role(g, y)
                    if kind == step:
                        for j in range(2):
                            gram_ref[tile(nf, j, ra, cb)] = fin[g, y, j].astype(F32)
            for g in range(SETS):
                for y in range(NY):
                    nf, kind, ra, cb = role(g, y)
                    for j in range(2):
                        if kind == 1 and step == 3:
                            gram_ref[tile(nf, j, cb, ra)] = fin[g, y, 2 + j].astype(F32)
                        if kind == 2 and step == 2:
                            gram_ref[tile(nf, j, cb, ra)] += fin[g, y, 2 + j].astype(F32)


def local(snapshots, var_index, modes, retained):
    rows, cols = snapshots.shape
    n_space, n_time = lax.axis_size("space"), lax.axis_size("tm")
    total_rows = rows * n_space
    count = float(total_rows // VARS * (cols * n_time))
    root = float(total_rows) ** 0.5
    r = modes.shape[1]
    fk = (rows // 128 + 1) // 2 * 128
    dma = pltpu.SemaphoreType.DMA

    def body(*refs):
        kernel(count, root, fk, *refs)

    vmem = pl.BlockSpec(memory_space=pltpu.VMEM)
    nparts = len(CUTS) - 1
    fin, red = pl.pallas_call(
        body,
        name="gram",
        out_shape=(jax.ShapeDtypeStruct((SETS, NY, 4, 128, 128), BF16), jax.ShapeDtypeStruct((r // n_space, cols), F32)),
        in_specs=[vmem, vmem, vmem, pl.BlockSpec(memory_space=pltpu.SMEM)],
        out_specs=(pl.BlockSpec(memory_space=pl.ANY), vmem),
        scratch_shapes=[
            pltpu.VMEM((cols, rows), BF16),
            pltpu.VMEM((3, cols, rows), BF16),
            pltpu.VMEM((cols, rows), BF16),
            pltpu.VMEM((cols, fk), BF16),
            pltpu.VMEM((cols, fk), BF16),
            pltpu.VMEM((2, cols, rows), BF16),
            pltpu.VMEM((2, 2, 128, rows), BF16),
            pltpu.VMEM((2, 256, rows), BF16),
            pltpu.VMEM((VARS, rows), F32),
            pltpu.VMEM((1, rows), F32),
            pltpu.VMEM((1, rows), F32),
            pltpu.VMEM((r, rows), BF16),
            pltpu.VMEM((24, 128), F32),
            pltpu.VMEM((24, 128), F32),
            pltpu.VMEM((7, 24, 128), F32),
            pltpu.VMEM((15, 24, 128), F32),
            pltpu.VMEM((SETS, NY, 2, 128, 128), F32),
            pltpu.VMEM((SETS, NY, 2, 128, 128), BF16),
            pltpu.VMEM((EARLY, NY - 1, 2, 128, 128), BF16),
            pltpu.VMEM((EARLY, 2, 128, 128), F32),
            pltpu.VMEM((EARLY, 128, 128), F32),
            pltpu.VMEM((r, cols), F32),
            pltpu.VMEM((7, 8, cols), F32),
            pltpu.VMEM((SETS, 128, 128), BF16),
            pltpu.VMEM((SETS, 128, 128), BF16),
            dma((6, nparts)), dma((6, nparts)), dma((7,)), dma((7,)), dma((15,)), dma((15,)),
            dma((EARLY, 3)), dma((EARLY, 3)), dma((EARLY,)), dma((EARLY,)), dma((7,)), dma((7,)),
            dma((SETS, 4)), dma((SETS, 4)), dma((SETS, 3)), dma((SETS, NY)),
            dma((SETS, NY, 2)), dma((SETS, NY, 2)), dma((SETS, NY, 4)),
            pltpu.VMEM((SETS - EARLY, 7, 128, 128), BF16), dma((SETS - EARLY, 7)), dma((SETS - EARLY, 7)),
        ],
        compiler_params=pltpu.CompilerParams(
            collective_id=0, has_side_effects=True, vmem_limit_bytes=60 * 2 ** 20),
    )(snapshots, var_index, modes.T, retained)
    t = lax.axis_index("tm")
    spot = jnp.stack([(t // 2) % NX, t // 8])
    gram, red = pl.pallas_call(
        assemble,
        name="columns",
        grid_spec=pltpu.PrefetchScalarGridSpec(
            num_scalar_prefetch=1,
            grid=(NX,),
            in_specs=[pl.BlockSpec(fin.shape, lambda k, p: (0,) * 5), pl.BlockSpec(red.shape, lambda k, p: (0, 0))],
            out_specs=[pl.BlockSpec((2, 1, 2 * cols, cols), lambda k, p: (0, (p[0] + k) % NX, 0, 0)),
                       pl.BlockSpec(red.shape, lambda k, p: (0, 0))],
        ),
        out_shape=(jax.ShapeDtypeStruct((2, NX, 2 * cols, cols), F32), jax.ShapeDtypeStruct(red.shape, F32)),
        compiler_params=pltpu.CompilerParams(vmem_limit_bytes=60 * 2 ** 20),
    )(spot, fin, red)
    return gram.reshape(cols * n_time, cols), red


def solution(mesh):
    return jax.shard_map(
        local,
        mesh=mesh,
        in_specs=(P("space", "tm"), P("space"), P("space", None), P()),
        out_specs=(P(None, "tm"), P("space", "tm")),
        check_vma=False,
    )
```

time: 126 us -> 105 us (0.83)
  the two profiles are of different devices: /device:TPU:54 before, /device:TPU:1 now
where the time goes in v3:
time: 105 us
  Pallas kernels  103 us (98%)
  between operations  1.32 us (1%)
    pallas_call x1, Pallas kernels, local(): pl.pallas_call(body, name='gram', out_shape=(jax.ShapeDtypeStruct((SETS,...  98.2 us
    pallas_call x1, Pallas kernels, local(): pl.pallas_call(assemble, name='columns', grid_spec=pltpu.PrefetchScalarGr...  5.16 us

profile of v3, /device:TPU:1, one launch (start us, length us, event | category | flops | bytes accessed | tf_op | source)
XLA Modules:
  0.0 105.3 jit_solution(1464448230381275222)
XLA Ops:
  1.3 0.6 pad_add_fusion.place_ref
  1.9 98.2 %gram.1 = (bf16[6,4,4,128,128]{4,3,2,1,0:T(8,128)(2,1)}, f32[8,256]{1,0:T(8,128)}) custom-call(bf16[3200,256]{1,0:T(8,128)(2,1)} %refs_0_.1, s32[3200]{0:T(1024)} %refs_1_.1, bf16[64,3200]{1,0:T(8,128)(2,1)} %bitcast.4, s32[1]{0:T(128)S(6)} %copy.6.refs_3_), custom_call_target="tpu_custom_call" | custom-call | tf_op jit(solution)/shard_map/gram/pallas_call | solution.py:559
  100.1 5.2 %columns.1 = (f32[2,4,512,256]{3,2,1,0:T(8,128)}, f32[8,256]{1,0:T(8,128)}) custom-call(s32[2]{0:T(128)} %pad_add_fusion.place_ref, bf16[6,4,4,128,128]{4,3,2,1,0:T(8,128)(2,1)} %get-tuple-element.6.fin, f32[8,256]{1,0:T(8,128)} %get-tuple-element.7.red_in), custom_call_target="tpu_custom_call" | custom-call | tf_op jit(solution)/shard_map/columns/pallas_call | solution.py:602

commit v4 on v3

--- a/solution.py
+++ b/solution.py
@@ -24,14 +24,19 @@
     return lax.dot_general(a, b, (((1,), (1,)), ((), ())), preferred_element_type=F32)
 
 
+def pack(n, total, squares):
+    lane = lax.broadcasted_iota(jnp.int32, (VARS, 128), 1)
+    return jnp.where(lane == 0, n, jnp.where(lane == 1, total, squares))
+
+
 def merge(tiles):
-    n = sum(t[0:8] for t in tiles)
-    total = sum(t[8:16] for t in tiles)
+    n = sum(t[:, 0:1] for t in tiles)
+    total = sum(t[:, 1:2] for t in tiles)
     mean = total / jnp.maximum(n, 1.0)
     squares = jnp.zeros_like(n)
     for t in tiles:
-        off = t[8:16] / jnp.maximum(t[0:8], 1.0) - mean
-        squares = squares + t[16:24] + t[0:8] * off * off
+        off = t[:, 1:2] / jnp.maximum(t[:, 0:1], 1.0) - mean
+        squares = squares + t[:, 2:3] + t[:, 0:1] * off * off
     return n, total, squares
 
 
@@ -50,8 +55,8 @@
 SETS = 6
 MIXED = (2, 5)
 EARLY = 3
-YFIRST = (3, 5)
-CUTS = (0, 32, 128, 160, 192, 224, 256)
+YFIRST = (3, 4)
+CUTS = (0, 16, 64, 128, 160, 192, 224, 256)
 ZCUTS = (0, 64, 128, 160, 192, 224, 256)
 
 
@@ -110,6 +115,11 @@
         to_diag.append(remote(raw.at[1, r], raw.at[2, r], bulk_s.at[4, k], bulk_r.at[4, k], core))
     to_core = remote(xt, raw.at[0], bulk_s.at[3, 0], bulk_r.at[3, 0], core)
 
+    def pass_f(*ks):
+        for k in ks:
+            to_f[k].wait_recv()
+            go(fwd[k])
+
     go(to_f[0], to_e[0], to_z[0])
     turn(1)
     go(to_core)
@@ -123,9 +133,6 @@
         acc = lax.fori_loop(0, cols // 16, body, jnp.zeros((16, rows), F32))
         return jnp.sum(acc, axis=0, keepdims=True)
 
-    def wide(v):
-        return jnp.broadcast_to(v, (VARS, 128))
-
     n1 = jnp.sum(hot[...], axis=1, keepdims=True) * cols
     sum1 = jnp.sum(hot[...] * colsum(lambda b: b), axis=1, keepdims=True)
     m1 = sum1 / jnp.maximum(n1, 1.0)
@@ -135,36 +142,30 @@
         d = b - mean_l[...]
         return d * d
     sq1 = jnp.sum(hot[...] * colsum(sq), axis=1, keepdims=True)
-    tile1[0:8] = wide(n1)
-    tile1[8:16] = wide(sum1)
-    tile1[16:24] = wide(sq1)
+    tile1[...] = pack(n1, sum1, sq1)
     sends1 = [remote(tile1, got1.at[i], st1_s.at[i], st1_r.at[i], dev1(*d)) for i, d in enumerate(ring1)]
     go(*sends1)
-    go(to_f[1], to_e[1])
+    go(to_f[1], to_e[1], to_f[2], to_e[2])
     keep = lax.broadcasted_iota(jnp.int32, kept.shape, 0) < ret_ref[0]
     kept[...] = jnp.where(keep, modes_ref[...].astype(F32), 0.0).astype(BF16)
     for half in range(2):
         ef[half, 128:256, :] = jnp.zeros((128, rows), BF16)
     for cp in sends1:
         cp.wait_recv()
-    to_f[0].wait_recv()
-    go(fwd[0])
+    pass_f(0)
     n2, sum2, sq2 = merge([tile1[...]] + [got1[i] for i in range(len(ring1))])
-    tile2[0:8] = n2
-    tile2[8:16] = sum2
-    tile2[16:24] = sq2
+    tile2[...] = pack(n2, sum2, sq2)
     sends2 = [remote(tile2, got2.at[i], st2_s.at[i], st2_r.at[i], dev2(*d)) for i, d in enumerate(ring2)]
     go(*sends2)
     go(to_z[1])
-    to_f[1].wait_recv()
-    go(fwd[1], to_e[2], *to_f[2:])
+    pass_f(1)
     for cp in sends2:
         cp.wait_recv()
     _, sum3, sq3 = merge([tile2[...]] + [got2[i] for i in range(len(ring2))])
     mean = sum3 / count
     inv = 1.0 / jnp.sqrt(sq3 / count + 1e-06)
-    mean_l[...] = jnp.sum(hot[...] * mean[:, 0:1], axis=0, keepdims=True)
-    inv_l[...] = jnp.sum(hot[...] * inv[:, 0:1], axis=0, keepdims=True)
+    mean_l[...] = jnp.sum(hot[...] * mean, axis=0, keepdims=True)
+    inv_l[...] = jnp.sum(hot[...] * inv, axis=0, keepdims=True)
     go(to_z[2])
 
     def scale_to(dst, dlo, src, lo, n, m, v):
@@ -188,13 +189,20 @@
         scale_to(ef.at[half, :, fl], 128 + lo, rawf, CUTS[k], CUTS[k + 1] - CUTS[k], mean_l[:, fl],
                  jnp.where(drop, 0.0, inv_l[:, fl]))
 
+    def pass_z(k):
+        to_z[k].wait_recv()
+        go(to_diag[k])
+
     def scale_z(k):
         half, lo, n = ZCUTS[k] // 128, ZCUTS[k] % 128, ZCUTS[k + 1] - ZCUTS[k]
-        to_z[k].wait_recv()
-        go(to_diag[k])
         scale(far.at[half, c], lo, raw.at[1], ZCUTS[k], n)
         to_diag[k].wait_recv()
         scale(far.at[half, 1 - c], lo, raw.at[2], ZCUTS[k], n)
+
+    def take_f(*ks):
+        for k in ks:
+            fwd[k].wait_recv()
+            scale_f(k)
 
     def scale_e(k):
         half, lo, n = CUTS[k] // 128, CUTS[k] % 128, CUTS[k + 1] - CUTS[k]
@@ -430,7 +438,10 @@
                             turned_y(g, 0).wait_send()
             under(cond, wait)
 
+    pass_f(2)
+    go(to_e[3], to_e[4], *to_f[3:])
     scale(near.at[c], 0, xt, 0, cols)
+    pass_z(0)
     to_core.wait_recv()
     scale(near.at[1 - c], 0, raw.at[0], 0, cols)
     near_own()
@@ -443,64 +454,61 @@
                             at(tl, ty, h, x, c)))
     go(*dsend)
     scale_e(0)
+    scale_e(1)
     scale_z(0)
+    pass_z(1)
     sum_l_start(0)
-    scale_z(1)
-    go(to_e[3], to_z[3])
-    far_with(2, 0, 0, near[c])
-    scale_e(1)
-    for k in range(2):
-        fwd[k].wait_recv()
-        scale_f(k)
+    go(to_z[3], to_e[5], to_e[6])
+    scale_e(2)
+    take_f(0, 1, 2)
     near_ef(1, 0)
     sum_y_start(1)
+    scale_z(1)
+    far_with(2, 0, 0, near[c])
     far_with(2, 2, 0, ef[0])
     sum_y_start(2)
     publish(0)
-    to_f[2].wait_recv()
-    go(fwd[2])
+    go(to_z[4])
+    pass_f(3)
+    pass_z(2)
+    scale_e(3)
     scale_z(2)
-    scale_e(2)
+    pass_f(4)
     sum_l_start(1)
+    pass_z(3)
+    pass_f(5)
+    scale_z(3)
     sum_l_start(2)
-    go(to_e[4], to_z[4])
-    to_f[3].wait_recv()
-    go(fwd[3])
-    scale_z(3)
-    scale_e(3)
+    go(to_z[5])
+    pass_f(6)
+    scale_e(4)
     spread(0)
+    take_f(3, 4)
     publish(1)
     publish(2)
-    go(to_e[5], to_z[5])
-    for k in (4, 5):
-        to_f[k].wait_recv()
-        go(fwd[k])
-    for k in (2, 3):
-        fwd[k].wait_recv()
-        scale_f(k)
+    scale_e(5)
+    scale_e(6)
+    pass_z(4)
+    take_f(5, 6)
+    near_ef(3, 1)
+    sum_start(3)
     scale_z(4)
-    scale_e(4)
+    far_with(4, 0, 0, ef[1])
+    pass_z(5)
     spread(1)
-    spread(2)
     scale_z(5)
     far_with(4, 2, 1, ef[0])
+    sum_start(4)
     far_with(5, 0, 1, near[c])
-    scale_e(5)
-    for k in (4, 5):
-        fwd[k].wait_recv()
-        scale_f(k)
-    near_ef(3, 1)
-    sum_start(3)
-    far_with(4, 0, 0, ef[1])
-    sum_start(4)
     far_with(5, 2, 1, ef[1])
     sum_start(5)
     publish_late(3)
-    publish(4)
+    publish_late(4)
+    spread(2)
+    publish(5)
     spread_late(3)
-    publish_late(5)
-    spread(4)
-    spread_late(5)
+    spread_late(4)
+    spread(5)
     for a in dsend:
         a.wait_recv()
     tot = redp[pl.ds(pl.multiple_of(s * 8, 8), 8), :]
@@ -514,31 +522,37 @@
         cp.wait_send()
 
 
-def assemble(place_ref, fin, red_in, gram_ref, red_ref):
-    k = pl.program_id(0)
-    h = place_ref[1]
+def assemble(fin, red_in, gram, red_ref, held, block, in_sem, out_sem):
+    _, _, h, x, _ = place()
+    loads = [pltpu.make_async_copy(fin.at[g], held.at[g], in_sem.at[g]) for g in range(SETS)]
+    for cp in loads:
+        cp.start()
     red_ref[...] = red_in[...]
 
-    def tile(nf, block, row, col):
-        return (h + nf) % 2, 0, pl.ds(block * 256 + row * 128, 128), pl.ds(col * 128, 128)
-
-    for step in range(NX):
-        @pl.when(k == step)
-        def _():
+    def tile(step, nf, half, row, col):
+        return step, (h + nf) % 2, pl.ds(half * 256 + row * 128, 128), pl.ds(col * 128, 128)
+
+    for cp in loads:
+        cp.wait()
+    for step in (0, 1, 3, 2):
+        for g in range(SETS):
+            for y in range(NY):
+                nf, kind, ra, cb = role(g, y)
+                for j in range(2):
+                    if kind == step:
+                        block[tile(step, nf, j, ra, cb)] = held[g, y, j].astype(F32)
+                    if kind == 1 and step == 3:
+                        block[tile(step, nf, j, cb, ra)] = held[g, y, 2 + j].astype(F32)
+        if step == 2:
             for g in range(SETS):
                 for y in range(NY):
                     nf, kind, ra, cb = role(g, y)
-                    if kind == step:
+                    if kind == 2:
                         for j in range(2):
-                            gram_ref[tile(nf, j, ra, cb)] = fin[g, y, j].astype(F32)
-            for g in range(SETS):
-                for y in range(NY):
-                    nf, kind, ra, cb = role(g, y)
-                    for j in range(2):
-                        if kind == 1 and step == 3:
-                            gram_ref[tile(nf, j, cb, ra)] = fin[g, y, 2 + j].astype(F32)
-                        if kind == 2 and step == 2:
-                            gram_ref[tile(nf, j, cb, ra)] += fin[g, y, 2 + j].astype(F32)
+                            block[tile(step, nf, j, cb, ra)] += held[g, y, 2 + j].astype(F32)
+        pltpu.make_async_copy(block.at[step], gram.at[:, (x + step) % NX], out_sem.at[step]).start()
+    for step in range(NX):
+        pltpu.make_async_copy(block.at[step], gram.at[:, (x + step) % NX], out_sem.at[step]).wait()
 
 
 def local(snapshots, var_index, modes, retained):
@@ -575,10 +589,10 @@
             pltpu.VMEM((1, rows), F32),
             pltpu.VMEM((1, rows), F32),
             pltpu.VMEM((r, rows), BF16),
-            pltpu.VMEM((24, 128), F32),
-            pltpu.VMEM((24, 128), F32),
-            pltpu.VMEM((7, 24, 128), F32),
-            pltpu.VMEM((15, 24, 128), F32),
+            pltpu.VMEM((VARS, 128), F32),
+            pltpu.VMEM((VARS, 128), F32),
+            pltpu.VMEM((7, VARS, 128), F32),
+            pltpu.VMEM((15, VARS, 128), F32),
             pltpu.VMEM((SETS, NY, 2, 128, 128), F32),
             pltpu.VMEM((SETS, NY, 2, 128, 128), BF16),
             pltpu.VMEM((EARLY, NY - 1, 2, 128, 128), BF16),
@@ -597,21 +611,15 @@
         compiler_params=pltpu.CompilerParams(
             collective_id=0, has_side_effects=True, vmem_limit_bytes=60 * 2 ** 20),
     )(snapshots, var_index, modes.T, retained)
-    t = lax.axis_index("tm")
-    spot = jnp.stack([(t // 2) % NX, t // 8])
     gram, red = pl.pallas_call(
         assemble,
         name="columns",
-        grid_spec=pltpu.PrefetchScalarGridSpec(
-            num_scalar_prefetch=1,
-            grid=(NX,),
-            in_specs=[pl.BlockSpec(fin.shape, lambda k, p: (0,) * 5), pl.BlockSpec(red.shape, lambda k, p: (0, 0))],
-            out_specs=[pl.BlockSpec((2, 1, 2 * cols, cols), lambda k, p: (0, (p[0] + k) % NX, 0, 0)),
-                       pl.BlockSpec(red.shape, lambda k, p: (0, 0))],
-        ),
+        in_specs=[pl.BlockSpec(memory_space=pl.ANY), vmem],
+        out_specs=(pl.BlockSpec(memory_space=pl.ANY), vmem),
         out_shape=(jax.ShapeDtypeStruct((2, NX, 2 * cols, cols), F32), jax.ShapeDtypeStruct(red.shape, F32)),
+        scratch_shapes=[pltpu.VMEM(fin.shape, BF16), pltpu.VMEM((NX, 2, 2 * cols, cols), F32), dma((SETS,)), dma((NX,))],
         compiler_params=pltpu.CompilerParams(vmem_limit_bytes=60 * 2 ** 20),
-    )(spot, fin, red)
+    )(fin, red)
     return gram.reshape(cols * n_time, cols), red
 
 

time: 105 us -> 99.3 us (0.946)
  Pallas kernels: 103 us -> 97.8 us
    pallas_call x1, Pallas kernels: 98.2 us -> 92.5 us  [local(): pl.pallas_call(body, name='gram', out_shape=(jax.ShapeDtypeStruct((SETS,...]
where the time goes in v4:
time: 99.3 us; the launch traced here: 99.1 us
  Pallas kernels  97.8 us (98%)
  between operations  1.28 us (1%)
    pallas_call x1, Pallas kernels, local(): pl.pallas_call(body, name='gram', out_shape=(jax.ShapeDtypeStruct((SETS,...  92.5 us
    pallas_call x1, Pallas kernels, local(): pl.pallas_call(assemble, name='columns', in_specs=[pl.BlockSpec(memory_sp...  5.29 us

profile of v4, /device:TPU:1, one launch (start us, length us, event | category | flops | bytes accessed | tf_op | source)
XLA Modules:
  0.0 99.1 jit_solution(9525500508716319235)
XLA Ops:
  1.3 92.5 %gram.1 = (bf16[6,4,4,128,128]{4,3,2,1,0:T(8,128)(2,1)}, f32[8,256]{1,0:T(8,128)}) custom-call(bf16[3200,256]{1,0:T(8,128)(2,1)} %refs_0_.1, s32[3200]{0:T(1024)} %refs_1_.1, bf16[64,3200]{1,0:T(8,128)(2,1)} %bitcast.2, s32[1]{0:T(128)S(6)} %copy.6.refs_3_), custom_call_target="tpu_custom_call" | custom-call | tf_op jit(solution)/shard_map/gram/pallas_call | solution.py:573
  93.8 5.3 %columns.1 = (f32[2,4,512,256]{3,2,1,0:T(8,128)}, f32[8,256]{1,0:T(8,128)}) custom-call(bf16[6,4,4,128,128]{4,3,2,1,0:T(8,128)(2,1)} %get-tuple-element.6.fin, f32[8,256]{1,0:T(8,128)} %get-tuple-element.7.red_in), custom_call_target="tpu_custom_call" | custom-call | tf_op jit(solution)/shard_map/columns/pallas_call | solution.py:614

commit v5 on v4

--- a/solution.py
+++ b/solution.py
@@ -55,7 +55,8 @@
 SETS = 6
 MIXED = (2, 5)
 EARLY = 3
-YFIRST = (3, 4)
+YFIRST = (1, 2, 5)
+ZFIRST = (0, 3, 4)
 CUTS = (0, 16, 64, 128, 160, 192, 224, 256)
 ZCUTS = (0, 64, 128, 160, 192, 224, 256)
 
@@ -63,14 +64,12 @@
 def kernel(count, root, fk, x_ref, vi_ref, modes_ref, ret_ref, fin, red_ref,
            xt, raw, rawe, relay, rawf, near, far, ef, hot, mean_l, inv_l, kept,
            tile1, tile2, got1, got2, ps, cs, rs, tmp, r2, redp, redr, pc, pt,
-           bulk_s, bulk_r, st1_s, st1_r, st2_s, st2_r, rs_s, rs_r, r2_s, r2_r, rd_s, rd_r, a_s, fin_r, b_s, b_r,
-           ay_s, al_s, late_r, rd, d_s, d_r):
+           rd, bulk_s, bulk_r, st_s, st_r, rs_s, rs_r, r2_s, r2_r, d_s, d_r, zf_s, zf_r, yf_s, yf_r):
     l, y, h, x, c = place()
     s = l * NY + y
     rows = xt.shape[1]
     cols = xt.shape[0]
     ntile = rows // 128
-    drain = []
 
     ring1 = [(dx, dc) for dx in range(NX) for dc in range(2) if (dx, dc) != (0, 0)]
     ring2 = [(dy, dl, dh) for dy in range(NY) for dl in range(2) for dh in range(2) if (dy, dl, dh) != (0, 0, 0)]
@@ -100,20 +99,23 @@
     def go(*copies):
         for cp in copies:
             cp.start()
-            drain.append(cp)
+
+    def got(ref, sem):
+        pltpu.make_async_copy(ref, ref, sem).wait()
 
     fs_mine = pl.multiple_of((x // 2) * (rows - fk), 128)
     parts = [pl.ds(lo, hi - lo) for lo, hi in zip(CUTS, CUTS[1:])]
     to_f, to_e, to_z, to_core, to_diag, fwd = [], [], [], [], [], []
     left, core = at(l, y, h, (x + NX - 1) % NX, c), at(l, y, h, x, 1 - c)
+    nf, nz = len(CUTS) - 1, len(ZCUTS) - 1
     for k, r in enumerate(parts):
-        to_f.append(remote(xt.at[r, pl.ds(fs_mine, fk)], relay.at[r], bulk_s.at[0, k], bulk_r.at[0, k], left))
-        to_e.append(remote(xt.at[r], rawe.at[r], bulk_s.at[1, k], bulk_r.at[1, k], at(l, y, h, (x + 1) % NX, c)))
-        fwd.append(remote(relay.at[r], rawf.at[r], bulk_s.at[5, k], bulk_r.at[5, k], left))
+        to_f.append(remote(xt.at[r, pl.ds(fs_mine, fk)], relay.at[r], bulk_s.at[0], bulk_r.at[k], left))
+        to_e.append(remote(xt.at[r], rawe.at[r], bulk_s.at[1], bulk_r.at[nf + k], at(l, y, h, (x + 1) % NX, c)))
+        fwd.append(remote(relay.at[r], rawf.at[r], bulk_s.at[5], bulk_r.at[2 * nf + k], left))
     for k, r in enumerate([pl.ds(lo, hi - lo) for lo, hi in zip(ZCUTS, ZCUTS[1:])]):
-        to_z.append(remote(xt.at[r], raw.at[1, r], bulk_s.at[2, k], bulk_r.at[2, k], at(l, y, 1 - h, x, c)))
-        to_diag.append(remote(raw.at[1, r], raw.at[2, r], bulk_s.at[4, k], bulk_r.at[4, k], core))
-    to_core = remote(xt, raw.at[0], bulk_s.at[3, 0], bulk_r.at[3, 0], core)
+        to_z.append(remote(xt.at[r], raw.at[1, r], bulk_s.at[2], bulk_r.at[3 * nf + k], at(l, y, 1 - h, x, c)))
+        to_diag.append(remote(raw.at[1, r], raw.at[2, r], bulk_s.at[4], bulk_r.at[3 * nf + nz + k], core))
+    to_core = remote(xt, raw.at[0], bulk_s.at[3], bulk_r.at[3 * nf + 2 * nz], core)
 
     def pass_f(*ks):
         for k in ks:
@@ -143,24 +145,22 @@
         return d * d
     sq1 = jnp.sum(hot[...] * colsum(sq), axis=1, keepdims=True)
     tile1[...] = pack(n1, sum1, sq1)
-    sends1 = [remote(tile1, got1.at[i], st1_s.at[i], st1_r.at[i], dev1(*d)) for i, d in enumerate(ring1)]
+    sends1 = [remote(tile1, got1.at[i], st_s.at[0], st_r.at[0], dev1(*d)) for i, d in enumerate(ring1)]
     go(*sends1)
     go(to_f[1], to_e[1], to_f[2], to_e[2])
     keep = lax.broadcasted_iota(jnp.int32, kept.shape, 0) < ret_ref[0]
     kept[...] = jnp.where(keep, modes_ref[...].astype(F32), 0.0).astype(BF16)
     for half in range(2):
         ef[half, 128:256, :] = jnp.zeros((128, rows), BF16)
-    for cp in sends1:
-        cp.wait_recv()
+    got(got1, st_r.at[0])
     pass_f(0)
     n2, sum2, sq2 = merge([tile1[...]] + [got1[i] for i in range(len(ring1))])
     tile2[...] = pack(n2, sum2, sq2)
-    sends2 = [remote(tile2, got2.at[i], st2_s.at[i], st2_r.at[i], dev2(*d)) for i, d in enumerate(ring2)]
+    sends2 = [remote(tile2, got2.at[i], st_s.at[1], st_r.at[1], dev2(*d)) for i, d in enumerate(ring2)]
     go(*sends2)
     go(to_z[1])
     pass_f(1)
-    for cp in sends2:
-        cp.wait_recv()
+    got(got2, st_r.at[1])
     _, sum3, sq3 = merge([tile2[...]] + [got2[i] for i in range(len(ring2))])
     mean = sum3 / count
     inv = 1.0 / jnp.sqrt(sq3 / count + 1e-06)
@@ -231,14 +231,14 @@
         cs[g] = ps[g].astype(BF16)
         go(*sum_y[g])
 
-    sum_y = [[remote(cs.at[g, (y + dy) % NY], rs.at[g, dy - 1], rs_s.at[g, dy - 1], rs_r.at[g, dy - 1],
+    sum_y = [[remote(cs.at[g, (y + dy) % NY], rs.at[g, dy - 1], rs_s.at[g], rs_r.at[g],
                      at(l, (y + dy) % NY, h, x, c)) for dy in range(1, NY)] for g in range(EARLY)]
     sum_l = [remote(tmp.at[g, 1 - l], r2.at[g], r2_s.at[g], r2_r.at[g], at(1 - l, y, h, x, c)) for g in range(EARLY)]
 
     ring3 = [(dl, dy) for dl in range(2) for dy in range(NY) if (dl, dy) != (0, 0)]
     sum_s = {}
     for g in range(EARLY, SETS):
-        sum_s[g] = [remote(cs.at[g, (y + dy) % NY, (l + dl) % 2], rd.at[g - EARLY, i], d_s.at[g - EARLY, i], d_r.at[g - EARLY, i],
+        sum_s[g] = [remote(cs.at[g, (y + dy) % NY, (l + dl) % 2], rd.at[g - EARLY, i], d_s.at[g - EARLY], d_r.at[g - EARLY],
                            at((l + dl) % 2, (y + dy) % NY, h, x, c)) for i, (dl, dy) in enumerate(ring3)]
 
     def sum_start(g):
@@ -250,16 +250,14 @@
             sum_l[g].wait_recv()
             tot = tmp[g, l] + r2[g]
         else:
-            for cp in sum_s[g]:
-                cp.wait_recv()
+            got(rd.at[g - EARLY], d_r.at[g - EARLY])
             tot = ps[g, y, l]
             for i in range(len(ring3)):
                 tot = tot + rd[g - EARLY, i].astype(F32)
         return tot * (1.0 / root)
 
     def sum_l_start(g):
-        for cp in sum_y[g]:
-            cp.wait_recv()
+        got(rs.at[g], rs_r.at[g])
         tot = ps[g, y]
         for k in range(NY - 1):
             tot = tot + rs[g, k].astype(F32)
@@ -279,164 +277,112 @@
         else:
             pl.when(cond)(fn)
 
-    def asis(g, k, two):
-        xd = (x + 3 - y % 2) % NX if two else x
-        return remote(pc.at[g], fin.at[g, y, l], a_s.at[g, k], fin_r.at[g, l], at((l + k) % 2, y, h, xd, c))
-
-    def turned(g, k):
-        hd = (h + role(g, 3)[0]) % 2
-        return remote(pt.at[g], fin.at[g, y, 2 + c], a_s.at[g, 2 + k], fin_r.at[g, 2 + c], at((l + k) % 2, y, hd, x, l))
+    def slots(n):
+        return cs.at[0] if n == 8 else rd.at[0, pl.ds(0, n)]
 
     def publish(g):
+        zf = g in ZFIRST
+        i = (ZFIRST if zf else YFIRST).index(g)
+        send, cond_send = (zf_s.at[i, 0], zf_s.at[i, 1]) if zf else (yf_s.at[i, 0], yf_s.at[i, 1])
+        recv, recv_t = (zf_r.at[i, 0], zf_r.at[i, 0]) if zf else (yf_r.at[i, 0], yf_r.at[i, 1])
+        far_set = role(g, 3)[0]
+        spots = [((l + k) % 2, y) for k in range(2)] if zf else [(l, (y + k) % NY) for k in range(NY)]
         tot = total(g)
         pc[g] = tot.astype(BF16)
         if g > 0:
             pt[g] = tot.T.astype(BF16)
-        for cond, two in kinds(g):
-            def send(two=two):
-                if two:
-                    asis(g, 0, True).start()
-                    asis(g, 1, True).start()
-                    turned(g, 1).start()
-                    if role(g, 3)[0]:
-                        turned(g, 0).start()
-                    else:
-                        @pl.when(c == l)
-                        def _():
-                            pltpu.make_async_copy(pt.at[g], fin.at[g, y, 2 + c], fin_r.at[g, 2 + c]).start()
-
-                        @pl.when(c != l)
-                        def _():
-                            turned(g, 0).start()
-                else:
-                    pltpu.make_async_copy(pc.at[g], fin.at[g, y, l], fin_r.at[g, l]).start()
-                    asis(g, 1, False).start()
-            under(cond, send)
-
-    def along_y(g, dy, n):
-        return remote(fin.at[g, y, pl.ds(0, n)], fin.at[g, y, pl.ds(0, n)], b_s.at[g, dy - 1], b_r.at[g, y],
-                      at(l, (y + dy) % NY, h, x, c))
-
-    def got(ref, sem):
-        pltpu.make_async_copy(ref, ref, sem).wait()
-
-    def spread(g):
-        for cond, two in kinds(g):
-            def send(two=two):
-                n = 4 if two else 2
-                for k in range(n):
-                    got(fin.at[g, y, k], fin_r.at[g, k])
-                for dy in range(1, NY):
-                    along_y(g, dy, n).start()
-            under(cond, send)
-
-    def finish(g):
-        for j in range(NY):
-            n = 4 if role(g, j)[1] else 2
-
-            @pl.when(y != j)
-            def _():
-                got(fin.at[g, j, pl.ds(0, n)], b_r.at[g, j])
-        for cond, two in kinds(g):
-            def wait(two=two):
-                n = 4 if two else 2
-                for dy in range(1, NY):
-                    along_y(g, dy, n).wait_send()
-                if two:
-                    asis(g, 0, True).wait_send()
-                    asis(g, 1, True).wait_send()
-                    turned(g, 1).wait_send()
-                    if role(g, 3)[0]:
-                        turned(g, 0).wait_send()
-                    else:
-                        @pl.when(c != l)
-                        def _():
-                            turned(g, 0).wait_send()
-                else:
-                    asis(g, 1, False).wait_send()
-            under(cond, wait)
-
-    def asis_y(g, dy, two):
-        xd = (x + 3 - y % 2) % NX if two else x
-        return remote(pc.at[g], fin.at[g, y, l], ay_s.at[g, dy, 0], late_r.at[g, y, l], at(l, (y + dy) % NY, h, xd, c))
-
-    def turned_y(g, dy):
-        hd = (h + role(g, 3)[0]) % 2
-        return remote(pt.at[g], fin.at[g, y, 2 + c], ay_s.at[g, dy, 1], late_r.at[g, y, 2 + c],
-                      at(l, (y + dy) % NY, hd, x, l))
-
-    def publish_late(g):
-        tot = total(g)
-        pc[g] = tot.astype(BF16)
-        pt[g] = tot.T.astype(BF16)
-        for cond, two in kinds(g):
-            def send(two=two):
-                for dy in range(1, NY):
-                    asis_y(g, dy, two).start()
-                    if two:
-                        turned_y(g, dy).start()
-                if two:
-                    asis_y(g, 0, True).start()
-                    if role(g, 3)[0]:
-                        turned_y(g, 0).start()
-                    else:
-                        @pl.when(c == l)
-                        def _():
-                            pltpu.make_async_copy(pt.at[g], fin.at[g, y, 2 + c], late_r.at[g, y, 2 + c]).start()
-
-                        @pl.when(c != l)
-                        def _():
-                            turned_y(g, 0).start()
-                else:
-                    pltpu.make_async_copy(pc.at[g], fin.at[g, y, l], late_r.at[g, y, l]).start()
-            under(cond, send)
-
-    def across_asis(g, j):
-        return remote(fin.at[g, j, l], fin.at[g, j, l], al_s.at[g, j, 0], late_r.at[g, j, l], at(1 - l, y, h, x, c))
-
-    def across_turned(g, j):
-        pair = fin.at[g, j, pl.ds(2, 2)]
-        return remote(pair, pair, al_s.at[g, j, 1], late_r.at[g, j, 2], at(1 - l, y, h, x, c))
-
-    def spread_late(g):
-        for j in range(NY):
-            got(fin.at[g, j, l], late_r.at[g, j, l])
-            across_asis(g, j).start()
-        for j in range(NY):
-            if role(g, j)[1]:
+
+        def asis(k, xd):
+            return remote(pc.at[g], fin.at[g, y, l], send, recv, at(*spots[k], h, xd, c))
+
+        def turned(k, sem):
+            return remote(pt.at[g], fin.at[g, y, 2 + c], sem, recv_t, at(*spots[k], (h + far_set) % 2, x, l))
+
+        def start(two):
+            if not two:
+                pltpu.make_async_copy(pc.at[g], fin.at[g, y, l], recv).start()
+                for k in range(1, len(spots)):
+                    asis(k, x).start()
+                return
+            for k in range(len(spots)):
+                asis(k, (x + 3 - y % 2) % NX).start()
+                if k > 0:
+                    turned(k, send).start()
+            if far_set:
+                turned(0, send).start()
+            else:
                 @pl.when(c == l)
                 def _():
-                    for k in (2, 3):
-                        got(fin.at[g, j, k], late_r.at[g, j, k])
-                    across_turned(g, j).start()
-
-    def finish_late(g):
-        for j in range(NY):
-            got(fin.at[g, j, 1 - l], late_r.at[g, j, 1 - l])
-            across_asis(g, j).wait_send()
-            if role(g, j)[1]:
+                    pltpu.make_async_copy(pt.at[g], fin.at[g, y, 2 + c], recv_t).start()
+
                 @pl.when(c != l)
                 def _():
-                    got(fin.at[g, j, pl.ds(2, 2)], late_r.at[g, j, 2])
-
-                @pl.when(c == l)
+                    turned(0, cond_send).start()
+
+        def sent(two):
+            n = 2 * len(spots) if two else len(spots)
+            if not two or not far_set:
+                n -= 1
+            got(slots(n), send)
+            if two and not far_set:
+                @pl.when(c != l)
                 def _():
-                    across_turned(g, j).wait_send()
+                    turned(0, cond_send).wait_send()
+
         for cond, two in kinds(g):
-            def wait(two=two):
-                for dy in range(1, NY):
-                    asis_y(g, dy, two).wait_send()
-                    if two:
-                        turned_y(g, dy).wait_send()
-                if two:
-                    asis_y(g, 0, True).wait_send()
-                    if role(g, 3)[0]:
-                        turned_y(g, 0).wait_send()
-                    else:
-                        @pl.when(c != l)
-                        def _():
-                            turned_y(g, 0).wait_send()
-            under(cond, wait)
+            under(cond, lambda two=two: start(two))
+        wait_sent.append(lambda: [under(cond, lambda two=two: sent(two)) for cond, two in kinds(g)])
+
+    wait_sent = []
+
+    def along_y(g, dy):
+        i, n = ZFIRST.index(g), 4 if g > 0 else 2
+        mine = fin.at[g, y, pl.ds(0, n)]
+        return remote(mine, mine, zf_s.at[i, 2], zf_r.at[i, 1], at(l, (y + dy) % NY, h, x, c))
+
+    def spread(g):
+        n = 4 if g > 0 else 2
+        got(fin.at[g, y, pl.ds(0, n)], zf_r.at[ZFIRST.index(g), 0])
+        for dy in range(1, NY):
+            along_y(g, dy).start()
+
+    def finish(g):
+        i, n = ZFIRST.index(g), 4 if g > 0 else 2
+        three = fin.at[g, pl.ds(0, 3), pl.ds(0, n)]
+        got(three, zf_r.at[i, 1])
+        got(three, zf_s.at[i, 2])
+
+    def across(g, k):
+        i = YFIRST.index(g)
+        low = 2 if g in MIXED else 0
+        view = fin.at[g, pl.ds(0, NY), l] if k == 0 else fin.at[g, pl.ds(low, NY - low), pl.ds(2, 2)]
+        return remote(view, view, yf_s.at[i, 2 + k], yf_r.at[i, 2 if k == 0 else 1], at(1 - l, y, h, x, c)), view
+
+    def cross_asis(g):
+        cp, view = across(g, 0)
+        got(view, yf_r.at[YFIRST.index(g), 0])
+        cp.start()
+
+    def cross_turned(g):
+        @pl.when(c == l)
+        def _():
+            cp, view = across(g, 1)
+            got(view, yf_r.at[YFIRST.index(g), 1])
+            cp.start()
+
+    def finish_late(g):
+        i = YFIRST.index(g)
+        got(fin.at[g, pl.ds(0, NY), 1 - l], yf_r.at[i, 2])
+        cp, view = across(g, 1)
+
+        @pl.when(c != l)
+        def _():
+            got(view, yf_r.at[i, 1])
+
+        @pl.when(c == l)
+        def _():
+            cp.wait_send()
+        across(g, 0)[0].wait_send()
 
     pass_f(2)
     go(to_e[3], to_e[4], *to_f[3:])
@@ -450,7 +396,7 @@
     dsend = []
     for i, (dl, dy) in enumerate(ring3):
         tl, ty = (l + dl) % 2, (y + dy) % NY
-        dsend.append(remote(redp.at[pl.ds(pl.multiple_of((tl * NY + ty) * 8, 8), 8)], redr.at[i], rd_s.at[i], rd_r.at[i],
+        dsend.append(remote(redp.at[pl.ds(pl.multiple_of((tl * NY + ty) * 8, 8), 8)], redr.at[i], d_s.at[3], d_r.at[3],
                             at(tl, ty, h, x, c)))
     go(*dsend)
     scale_e(0)
@@ -495,22 +441,24 @@
     scale_z(4)
     far_with(4, 0, 0, ef[1])
     pass_z(5)
-    spread(1)
+    cross_asis(1)
     scale_z(5)
     far_with(4, 2, 1, ef[0])
     sum_start(4)
+    publish(3)
     far_with(5, 0, 1, near[c])
     far_with(5, 2, 1, ef[1])
     sum_start(5)
-    publish_late(3)
-    publish_late(4)
-    spread(2)
+    cross_turned(1)
+    spread(3)
+    publish(4)
+    cross_asis(2)
+    cross_turned(2)
     publish(5)
-    spread_late(3)
-    spread_late(4)
-    spread(5)
-    for a in dsend:
-        a.wait_recv()
+    spread(4)
+    cross_asis(5)
+    cross_turned(5)
+    got(redr, d_r.at[3])
     tot = redp[pl.ds(pl.multiple_of(s * 8, 8), 8), :]
     for i in range(len(ring3)):
         tot = tot + redr[i]
@@ -518,8 +466,20 @@
     for g in range(SETS):
         (finish_late if g in YFIRST else finish)(g)
 
-    for cp in drain:
-        cp.wait_send()
+    for fn in wait_sent:
+        fn()
+    own_f = remote(xt.at[:, pl.ds(fs_mine, fk)], relay, bulk_s.at[0], bulk_r.at[0], left)
+    own_f.wait_send()
+    for ref, k in ((xt, 1), (xt, 2), (xt, 3), (xt, 4), (relay, 5)):
+        got(ref, bulk_s.at[k])
+    got(got1, st_s.at[0])
+    got(got2, st_s.at[1])
+    for g in range(EARLY):
+        got(rs.at[g], rs_s.at[g])
+        sum_l[g].wait_send()
+    for g in range(SETS - EARLY):
+        got(rd.at[g], d_s.at[g])
+    got(redr, d_s.at[3])
 
 
 def assemble(fin, red_in, gram, red_ref, held, block, in_sem, out_sem):
@@ -569,7 +529,6 @@
         kernel(count, root, fk, *refs)
 
     vmem = pl.BlockSpec(memory_space=pltpu.VMEM)
-    nparts = len(CUTS) - 1
     fin, red = pl.pallas_call(
         body,
         name="gram",
@@ -602,11 +561,10 @@
             pltpu.VMEM((7, 8, cols), F32),
             pltpu.VMEM((SETS, 128, 128), BF16),
             pltpu.VMEM((SETS, 128, 128), BF16),
-            dma((6, nparts)), dma((6, nparts)), dma((7,)), dma((7,)), dma((15,)), dma((15,)),
-            dma((EARLY, 3)), dma((EARLY, 3)), dma((EARLY,)), dma((EARLY,)), dma((7,)), dma((7,)),
-            dma((SETS, 4)), dma((SETS, 4)), dma((SETS, 3)), dma((SETS, NY)),
-            dma((SETS, NY, 2)), dma((SETS, NY, 2)), dma((SETS, NY, 4)),
-            pltpu.VMEM((SETS - EARLY, 7, 128, 128), BF16), dma((SETS - EARLY, 7)), dma((SETS - EARLY, 7)),
+            pltpu.VMEM((SETS - EARLY, 7, 128, 128), BF16),
+            dma((6,)), dma((3 * (len(CUTS) - 1) + 2 * (len(ZCUTS) - 1) + 1,)), dma((2,)), dma((2,)),
+            dma((EARLY,)), dma((EARLY,)), dma((EARLY,)), dma((EARLY,)), dma((4,)), dma((4,)),
+            dma((3, 3)), dma((3, 2)), dma((3, 4)), dma((3, 3)),
         ],
         compiler_params=pltpu.CompilerParams(
             collective_id=0, has_side_effects=True, vmem_limit_bytes=60 * 2 ** 20),

time: 99.3 us -> 89.6 us (0.902)
  Pallas kernels: 97.8 us -> 88.1 us
    pallas_call x1, Pallas kernels: 92.5 us -> 82.8 us  [local(): pl.pallas_call(body, name='gram', out_shape=(jax.ShapeDtypeStruct((SETS,...]
where the time goes in v5:
time: 89.6 us; the launch traced here: 89.4 us
  Pallas kernels  88.1 us (98%)
  between operations  1.28 us (1%)
    pallas_call x1, Pallas kernels, local(): pl.pallas_call(body, name='gram', out_shape=(jax.ShapeDtypeStruct((SETS,...  82.8 us
    pallas_call x1, Pallas kernels, local(): pl.pallas_call(assemble, name='columns', in_specs=[pl.BlockSpec(memory_sp...  5.29 us

profile of v5, /device:TPU:1, one launch (start us, length us, event | category | flops | bytes accessed | tf_op | source)
XLA Modules:
  0.0 89.4 jit_solution(6440861640569499906)
XLA Ops:
  1.3 82.8 %gram.1 = (bf16[6,4,4,128,128]{4,3,2,1,0:T(8,128)(2,1)}, f32[8,256]{1,0:T(8,128)}) custom-call(bf16[3200,256]{1,0:T(8,128)(2,1)} %refs_0_.1, s32[3200]{0:T(1024)} %refs_1_.1, bf16[64,3200]{1,0:T(8,128)(2,1)} %bitcast.2, s32[1]{0:T(128)S(6)} %copy.6.refs_3_), custom_call_target="tpu_custom_call" | custom-call | tf_op jit(solution)/shard_map/gram/pallas_call | solution.py:532
  84.1 5.3 %columns.1 = (f32[2,4,512,256]{3,2,1,0:T(8,128)}, f32[8,256]{1,0:T(8,128)}) custom-call(bf16[6,4,4,128,128]{4,3,2,1,0:T(8,128)(2,1)} %get-tuple-element.6.fin, f32[8,256]{1,0:T(8,128)} %get-tuple-element.7.red_in), custom_call_target="tpu_custom_call" | custom-call | tf_op jit(solution)/shard_map/columns/pallas_call | solution.py:572

commit v6 on v5

--- a/solution.py
+++ b/solution.py
@@ -61,8 +61,8 @@
 ZCUTS = (0, 64, 128, 160, 192, 224, 256)
 
 
-def kernel(count, root, fk, x_ref, vi_ref, modes_ref, ret_ref, fin, red_ref,
-           xt, raw, rawe, relay, rawf, near, far, ef, hot, mean_l, inv_l, kept,
+def kernel(count, root, fk, x_hbm, vi_hbm, modes_hbm, ret_ref, fin, red_ref,
+           x_ref, vi_ref, modes_ref, load, xt, raw, rawe, relay, rawf, near, far, ef, hot, mean_l, inv_l, kept,
            tile1, tile2, got1, got2, ps, cs, rs, tmp, r2, redp, redr, pc, pt,
            rd, bulk_s, bulk_r, st_s, st_r, rs_s, rs_r, r2_s, r2_r, d_s, d_r, zf_s, zf_r, yf_s, yf_r):
     l, y, h, x, c = place()
@@ -80,6 +80,12 @@
     def dev2(dy, dl, dh):
         return at((l + dl) % 2, (y + dy) % NY, (h + dh) % 2, x, c)
 
+    lanes = [pl.ds(128 * half, 128) for half in range(2)]
+    x_loads = [pltpu.make_async_copy(x_hbm.at[:, r], x_ref.at[:, r], load.at[half]) for half, r in enumerate(lanes)]
+    vi_load = pltpu.make_async_copy(vi_hbm, vi_ref, load.at[2])
+    modes_load = pltpu.make_async_copy(modes_hbm, modes_ref, load.at[3])
+    for cp in x_loads + [vi_load, modes_load]:
+        cp.start()
     barrier = pltpu.get_barrier_semaphore()
     for d in ring1:
         pl.semaphore_signal(barrier, inc=1, device_id=dev1(*d), device_id_type=MESH)
@@ -87,6 +93,7 @@
         pl.semaphore_signal(barrier, inc=1, device_id=dev2(*d), device_id_type=MESH)
 
     def turn(half):
+        x_loads[half].wait()
         for k in range(ntile):
             xt[128 * half:128 * half + 128, 128 * k:128 * k + 128] = x_ref[128 * k:128 * k + 128, 128 * half:128 * half + 128].T
 
@@ -126,6 +133,7 @@
     turn(1)
     go(to_core)
 
+    vi_load.wait()
     hot[...] = (vi_ref[...][None, :] == lax.broadcasted_iota(jnp.int32, (VARS, rows), 0)).astype(F32)
 
     def colsum(fn):
@@ -148,6 +156,7 @@
     sends1 = [remote(tile1, got1.at[i], st_s.at[0], st_r.at[0], dev1(*d)) for i, d in enumerate(ring1)]
     go(*sends1)
     go(to_f[1], to_e[1], to_f[2], to_e[2])
+    modes_load.wait()
     keep = lax.broadcasted_iota(jnp.int32, kept.shape, 0) < ret_ref[0]
     kept[...] = jnp.where(keep, modes_ref[...].astype(F32), 0.0).astype(BF16)
     for half in range(2):
@@ -296,7 +305,10 @@
             return remote(pc.at[g], fin.at[g, y, l], send, recv, at(*spots[k], h, xd, c))
 
         def turned(k, sem):
-            return remote(pt.at[g], fin.at[g, y, 2 + c], sem, recv_t, at(*spots[k], (h + far_set) % 2, x, l))
+            tl, ty = spots[k]
+            if far_set and not zf:
+                tl = 1 - l
+            return remote(pt.at[g], fin.at[g, y, 2 + c], sem, recv_t, at(tl, ty, (h + far_set) % 2, x, l))
 
         def start(two):
             if not two:
@@ -363,8 +375,11 @@
         got(view, yf_r.at[YFIRST.index(g), 0])
         cp.start()
 
+    def first_hand(g):
+        return c != l if role(g, 3)[0] else c == l
+
     def cross_turned(g):
-        @pl.when(c == l)
+        @pl.when(first_hand(g))
         def _():
             cp, view = across(g, 1)
             got(view, yf_r.at[YFIRST.index(g), 1])
@@ -375,11 +390,11 @@
         got(fin.at[g, pl.ds(0, NY), 1 - l], yf_r.at[i, 2])
         cp, view = across(g, 1)
 
-        @pl.when(c != l)
+        @pl.when(jnp.logical_not(first_hand(g)))
         def _():
             got(view, yf_r.at[i, 1])
 
-        @pl.when(c == l)
+        @pl.when(first_hand(g))
         def _():
             cp.wait_send()
         across(g, 0)[0].wait_send()
@@ -445,16 +460,16 @@
     scale_z(5)
     far_with(4, 2, 1, ef[0])
     sum_start(4)
-    publish(3)
     far_with(5, 0, 1, near[c])
     far_with(5, 2, 1, ef[1])
+    publish(3)
     sum_start(5)
-    cross_turned(1)
     spread(3)
     publish(4)
+    cross_turned(1)
     cross_asis(2)
+    publish(5)
     cross_turned(2)
-    publish(5)
     spread(4)
     cross_asis(5)
     cross_turned(5)
@@ -482,37 +497,37 @@
     got(redr, d_s.at[3])
 
 
-def assemble(fin, red_in, gram, red_ref, held, block, in_sem, out_sem):
+def assemble(fin, red_in, gram, red_ref, block, out_sem):
     _, _, h, x, _ = place()
-    loads = [pltpu.make_async_copy(fin.at[g], held.at[g], in_sem.at[g]) for g in range(SETS)]
-    for cp in loads:
-        cp.start()
     red_ref[...] = red_in[...]
 
     def tile(step, nf, half, row, col):
         return step, (h + nf) % 2, pl.ds(half * 256 + row * 128, 128), pl.ds(col * 128, 128)
 
-    for cp in loads:
-        cp.wait()
+    def store(step, half):
+        return pltpu.make_async_copy(block.at[step, half], gram.at[half, (x + step) % NX], out_sem.at[2 * step + half])
+
     for step in (0, 1, 3, 2):
         for g in range(SETS):
             for y in range(NY):
                 nf, kind, ra, cb = role(g, y)
                 for j in range(2):
                     if kind == step:
-                        block[tile(step, nf, j, ra, cb)] = held[g, y, j].astype(F32)
+                        block[tile(step, nf, j, ra, cb)] = fin[g, y, j].astype(F32)
                     if kind == 1 and step == 3:
-                        block[tile(step, nf, j, cb, ra)] = held[g, y, 2 + j].astype(F32)
+                        block[tile(step, nf, j, cb, ra)] = fin[g, y, 2 + j].astype(F32)
         if step == 2:
             for g in range(SETS):
                 for y in range(NY):
                     nf, kind, ra, cb = role(g, y)
                     if kind == 2:
                         for j in range(2):
-                            block[tile(step, nf, j, cb, ra)] += held[g, y, 2 + j].astype(F32)
-        pltpu.make_async_copy(block.at[step], gram.at[:, (x + step) % NX], out_sem.at[step]).start()
+                            block[tile(step, nf, j, cb, ra)] += fin[g, y, 2 + j].astype(F32)
+        for half in range(2):
+            store(step, half).start()
     for step in range(NX):
-        pltpu.make_async_copy(block.at[step], gram.at[:, (x + step) % NX], out_sem.at[step]).wait()
+        for half in range(2):
+            store(step, half).wait()
 
 
 def local(snapshots, var_index, modes, retained):
@@ -532,10 +547,14 @@
     fin, red = pl.pallas_call(
         body,
         name="gram",
-        out_shape=(jax.ShapeDtypeStruct((SETS, NY, 4, 128, 128), BF16), jax.ShapeDtypeStruct((r // n_space, cols), F32)),
-        in_specs=[vmem, vmem, vmem, pl.BlockSpec(memory_space=pltpu.SMEM)],
-        out_specs=(pl.BlockSpec(memory_space=pl.ANY), vmem),
+        out_shape=(pltpu.VMEM((SETS, NY, 4, 128, 128), BF16), pltpu.VMEM((r // n_space, cols), F32)),
+        in_specs=[pl.BlockSpec(memory_space=pltpu.HBM)] * 3 + [pl.BlockSpec(memory_space=pltpu.SMEM)],
+        out_specs=(vmem, vmem),
         scratch_shapes=[
+            pltpu.VMEM((rows, cols), BF16),
+            pltpu.VMEM((rows,), jnp.int32),
+            pltpu.VMEM((r, rows), BF16),
+            dma((4,)),
             pltpu.VMEM((cols, rows), BF16),
             pltpu.VMEM((3, cols, rows), BF16),
             pltpu.VMEM((cols, rows), BF16),
@@ -567,16 +586,16 @@
             dma((3, 3)), dma((3, 2)), dma((3, 4)), dma((3, 3)),
         ],
         compiler_params=pltpu.CompilerParams(
-            collective_id=0, has_side_effects=True, vmem_limit_bytes=60 * 2 ** 20),
+            collective_id=0, has_side_effects=True, vmem_limit_bytes=59 * 2 ** 20),
     )(snapshots, var_index, modes.T, retained)
     gram, red = pl.pallas_call(
         assemble,
         name="columns",
-        in_specs=[pl.BlockSpec(memory_space=pl.ANY), vmem],
+        in_specs=[vmem, vmem],
         out_specs=(pl.BlockSpec(memory_space=pl.ANY), vmem),
         out_shape=(jax.ShapeDtypeStruct((2, NX, 2 * cols, cols), F32), jax.ShapeDtypeStruct(red.shape, F32)),
-        scratch_shapes=[pltpu.VMEM(fin.shape, BF16), pltpu.VMEM((NX, 2, 2 * cols, cols), F32), dma((SETS,)), dma((NX,))],
-        compiler_params=pltpu.CompilerParams(vmem_limit_bytes=60 * 2 ** 20),
+        scratch_shapes=[pltpu.VMEM((NX, 2, 2 * cols, cols), F32), dma((2 * NX,))],
+        compiler_params=pltpu.CompilerParams(vmem_limit_bytes=40 * 2 ** 20),
     )(fin, red)
     return gram.reshape(cols * n_time, cols), red
 

time: 89.6 us -> 84.6 us (0.944)
  Pallas kernels: 88.1 us -> 83.2 us
    pallas_call x2, Pallas kernels: 88.1 us -> 83.2 us  [the longest x1 80.4 us: local(): pl.pallas_call(body, name='gram', out_shape=(pltpu.VMEM((SETS, NY, 4, 128...]
where the time goes in v6:
time: 84.6 us; the launch traced here: 84.5 us
  Pallas kernels  83.2 us (98%)
  between operations  1.28 us (2%)
    pallas_call x1, Pallas kernels, local(): pl.pallas_call(body, name='gram', out_shape=(pltpu.VMEM((SETS, NY, 4, 128...  80.4 us
    pallas_call x1, Pallas kernels, local(): pl.pallas_call(assemble, name='columns', in_specs=[vmem, vmem], out_specs...  2.76 us

profile of v6, /device:TPU:1, one launch (start us, length us, event | category | flops | bytes accessed | tf_op | source)
XLA Modules:
  0.0 84.5 jit_solution(5528985424491798691)
XLA Ops:
  1.3 80.4 %gram.1 = (bf16[6,4,4,128,128]{4,3,2,1,0:T(8,128)(2,1)S(1)}, f32[8,256]{1,0:T(8,128)S(1)}) custom-call(bf16[3200,256]{1,0:T(8,128)(2,1)} %refs_0_.1, s32[3200]{0:T(1024)} %refs_1_.1, bf16[64,3200]{1,0:T(8,128)(2,1)} %bitcast.2, s32[1]{0:T(128)S(6)} %copy.6.refs_3_), custom_call_target="tpu_custom_call" | custom-call | tf_op jit(solution)/shard_map/gram/pallas_call | solution.py:547
  81.7 2.8 %columns.1 = (f32[2,4,512,256]{3,2,1,0:T(8,128)}, f32[8,256]{1,0:T(8,128)}) custom-call(bf16[6,4,4,128,128]{4,3,2,1,0:T(8,128)(2,1)S(1)} %get-tuple-element.6.fin, f32[8,256]{1,0:T(8,128)S(1)} %get-tuple-element.7.red_in), custom_call_target="tpu_custom_call" | custom-call | tf_op jit(solution)/shard_map/columns/pallas_call | solution.py:591

commit v7 on v6

--- a/solution.py
+++ b/solution.py
@@ -413,7 +413,6 @@
         tl, ty = (l + dl) % 2, (y + dy) % NY
         dsend.append(remote(redp.at[pl.ds(pl.multiple_of((tl * NY + ty) * 8, 8), 8)], redr.at[i], d_s.at[3], d_r.at[3],
                             at(tl, ty, h, x, c)))
-    go(*dsend)
     scale_e(0)
     scale_e(1)
     scale_z(0)
@@ -456,7 +455,7 @@
     scale_z(4)
     far_with(4, 0, 0, ef[1])
     pass_z(5)
-    cross_asis(1)
+    go(*dsend)
     scale_z(5)
     far_with(4, 2, 1, ef[0])
     sum_start(4)
@@ -464,6 +463,7 @@
     far_with(5, 2, 1, ef[1])
     publish(3)
     sum_start(5)
+    cross_asis(1)
     spread(3)
     publish(4)
     cross_turned(1)

time: 84.6 us -> 83.5 us (0.987)
  Pallas kernels: 83.2 us -> 82.1 us
    pallas_call x1, Pallas kernels: 80.4 us -> 79.4 us  [local(): pl.pallas_call(body, name='gram', out_shape=(pltpu.VMEM((SETS, NY, 4, 128...]
where the time goes in v7:
time: 83.5 us; the launch traced here: 83.4 us
  Pallas kernels  82.1 us (98%)
  between operations  1.28 us (2%)
    pallas_call x1, Pallas kernels, local(): pl.pallas_call(body, name='gram', out_shape=(pltpu.VMEM((SETS, NY, 4, 128...  79.4 us
    pallas_call x1, Pallas kernels, local(): pl.pallas_call(assemble, name='columns', in_specs=[vmem, vmem], out_specs...  2.76 us

profile of v7, /device:TPU:1, one launch (start us, length us, event | category | flops | bytes accessed | tf_op | source)
XLA Modules:
  0.0 83.4 jit_solution(4361011934895030048)
XLA Ops:
  1.3 79.4 %gram.1 = (bf16[6,4,4,128,128]{4,3,2,1,0:T(8,128)(2,1)S(1)}, f32[8,256]{1,0:T(8,128)S(1)}) custom-call(bf16[3200,256]{1,0:T(8,128)(2,1)} %refs_0_.1, s32[3200]{0:T(1024)} %refs_1_.1, bf16[64,3200]{1,0:T(8,128)(2,1)} %bitcast.2, s32[1]{0:T(128)S(6)} %copy.6.refs_3_), custom_call_target="tpu_custom_call" | custom-call | tf_op jit(solution)/shard_map/gram/pallas_call | solution.py:547
  80.6 2.8 %columns.1 = (f32[2,4,512,256]{3,2,1,0:T(8,128)}, f32[8,256]{1,0:T(8,128)}) custom-call(bf16[6,4,4,128,128]{4,3,2,1,0:T(8,128)(2,1)S(1)} %get-tuple-element.6.fin, f32[8,256]{1,0:T(8,128)S(1)} %get-tuple-element.7.red_in), custom_call_target="tpu_custom_call" | custom-call | tf_op jit(solution)/shard_map/columns/pallas_call | solution.py:591

commit v8 on v7

--- a/solution.py
+++ b/solution.py
@@ -241,10 +241,10 @@
         go(*sum_y[g])
 
     sum_y = [[remote(cs.at[g, (y + dy) % NY], rs.at[g, dy - 1], rs_s.at[g], rs_r.at[g],
-                     at(l, (y + dy) % NY, h, x, c)) for dy in range(1, NY)] for g in range(EARLY)]
+                     at(l, (y + dy) % NY, h, x, c)) for dy in (2, 1, 3)] for g in range(EARLY)]
     sum_l = [remote(tmp.at[g, 1 - l], r2.at[g], r2_s.at[g], r2_r.at[g], at(1 - l, y, h, x, c)) for g in range(EARLY)]
 
-    ring3 = [(dl, dy) for dl in range(2) for dy in range(NY) if (dl, dy) != (0, 0)]
+    ring3 = [(1, 2), (1, 1), (1, 3), (1, 0), (0, 2), (0, 1), (0, 3)]
     sum_s = {}
     for g in range(EARLY, SETS):
         sum_s[g] = [remote(cs.at[g, (y + dy) % NY, (l + dl) % 2], rd.at[g - EARLY, i], d_s.at[g - EARLY], d_r.at[g - EARLY],
@@ -355,7 +355,7 @@
     def spread(g):
         n = 4 if g > 0 else 2
         got(fin.at[g, y, pl.ds(0, n)], zf_r.at[ZFIRST.index(g), 0])
-        for dy in range(1, NY):
+        for dy in (2, 1, 3):
             along_y(g, dy).start()
 
     def finish(g):

time: 83.5 us -> 83.3 us (level)
  no operation moved by 1% of the time
where the time goes in v8:
time: 83.3 us; the launch traced here: 83.1 us
  Pallas kernels  81.9 us (98%)
  between operations  1.28 us (2%)
    pallas_call x1, Pallas kernels, local(): pl.pallas_call(body, name='gram', out_shape=(pltpu.VMEM((SETS, NY, 4, 128...  79.1 us
    pallas_call x1, Pallas kernels, local(): pl.pallas_call(assemble, name='columns', in_specs=[vmem, vmem], out_specs...  2.76 us

profile of v8, /device:TPU:1, one launch (start us, length us, event | category | flops | bytes accessed | tf_op | source)
XLA Modules:
  0.0 83.1 jit_solution(7357237002332840361)
XLA Ops:
  1.3 79.1 %gram.1 = (bf16[6,4,4,128,128]{4,3,2,1,0:T(8,128)(2,1)S(1)}, f32[8,256]{1,0:T(8,128)S(1)}) custom-call(bf16[3200,256]{1,0:T(8,128)(2,1)} %refs_0_.1, s32[3200]{0:T(1024)} %refs_1_.1, bf16[64,3200]{1,0:T(8,128)(2,1)} %bitcast.2, s32[1]{0:T(128)S(6)} %copy.6.refs_3_), custom_call_target="tpu_custom_call" | custom-call | tf_op jit(solution)/shard_map/gram/pallas_call | solution.py:547
  80.4 2.8 %columns.1 = (f32[2,4,512,256]{3,2,1,0:T(8,128)}, f32[8,256]{1,0:T(8,128)}) custom-call(bf16[6,4,4,128,128]{4,3,2,1,0:T(8,128)(2,1)S(1)} %get-tuple-element.6.fin, f32[8,256]{1,0:T(8,128)S(1)} %get-tuple-element.7.red_in), custom_call_target="tpu_custom_call" | custom-call | tf_op jit(solution)/shard_map/columns/pallas_call | solution.py:591
